TPU v7x, 512 devices: a whole 4x8x8 slice. The times are simulated.
512 devices in a mesh: grp: 8 (over y), row: 8 (over z), col: 8 (over x, core).
Axes of the slice: x: 4, y: 8, z: 8, core: 2. Of those that a mesh axis runs over, the one named last changes fastest.
Arguments:
- new_rows: bfloat16 [768, 16, 8192], P(('grp', 'col'), None, 'row'), may hold values from -6 to 6
- query_weight: bfloat16 [8192, 8192], P('row', 'col')
- key_weight: bfloat16 [8192, 1024], P('row', 'col')
- value_weight: bfloat16 [8192, 1024], P('row', 'col'), may hold values from -0.0625 to 0.0625
- cache_keys: bfloat16 [768, 512, 1024], P(('grp', 'row'), None, 'col'), may hold values from -6 to 6
- cache_values: bfloat16 [768, 512, 1024], P(('grp', 'row'), None, 'col'), may hold values from -6 to 6
- region_agents: int32 [768], replicated, may hold values from 0 to 767, as said below
- new_counts: int32 [768], replicated, may hold values from 4 to 16, as said below
- cache_lengths: int32 [768], replicated, may hold values from 1 to 512, as said below
Outputs:
- attended: bfloat16 [768, 16, 8192], P(('grp', 'col'), 'row')
Inputs may be any that keep to these rules, and one draw needn't show every extreme that they name: `region_agents`: A permutation of the 768 agents. Rows i with equal i // 12 form one region; agent a is served by group a // 96. Every region holds at most 3 agents served by one group, and exactly 3 of some group. `new_counts`: some agent has 16 new tokens. `cache_lengths`: some agent has 512 cached positions.
All inputs are finite; a program needn't handle non-finite values.
Results may differ from a plain program's by a relative error of at most 0.025.
Values may be sent and summed in bfloat16 or wider, within the bound.
A program may use at most 64 MiB of HBM per device.

v0:
```python
import jax
import jax.numpy as jnp
from jax import lax
from jax.sharding import PartitionSpec as P

HEAD_DIM = 128


rotary_base = 500000.0
floor_score = -1e30


def rotate_pairs(values, positions):
    half_dim = values.shape[-1] // 2
    exponent = jnp.arange(half_dim, dtype=jnp.float32) * (2.0 / values.shape[-1])
    frequency = rotary_base ** (-exponent)
    angles = positions.astype(jnp.float32)[..., None, None] * frequency
    cosine = jnp.cos(angles)
    sine_part = jnp.sin(angles)
    first_half = values[..., :half_dim]
    second = values[..., half_dim:]
    return jnp.concatenate(
        [first_half * cosine - second * sine_part, second * cosine + first_half * sine_part],
        axis=-1,
    )


def local(
    new_rows,
    query_weight,
    key_weight,
    value_weight,
    cache_keys,
    cache_values,
    region_agents,
    new_counts,
    cache_lengths,
):
    groups = lax.axis_size("grp")
    grid_rows = lax.axis_size("row")
    grid_cols = lax.axis_size("col")
    group_index = lax.axis_index("grp")
    row_index = lax.axis_index("row")
    col_index = lax.axis_index("col")
    agents_total = region_agents.shape[0]
    per_group = agents_total // groups
    per_region = new_rows.shape[0]
    regions = groups * grid_cols
    capacity = max(2, 2 * per_region // groups)
    slot_count = new_rows.shape[1]
    feature_width = new_rows.shape[2]
    slot_width = slot_count // grid_cols
    served_by = region_agents // per_group
    grouped = served_by.reshape(regions, per_region)
    earlier = jnp.arange(per_region)[:, None] > jnp.arange(per_region)[None, :]
    same_group = grouped[:, :, None] == grouped[:, None, :]
    bucket = jnp.sum((same_group & earlier[None, :, :]).astype(jnp.int32), axis=2).reshape(
        agents_total
    )
    slot_of_agent = jnp.argsort(region_agents)
    my_region = group_index * grid_cols + col_index
    mine_group = lax.dynamic_slice_in_dim(served_by, my_region * per_region, per_region)
    mine_bucket = lax.dynamic_slice_in_dim(bucket, my_region * per_region, per_region)
    choose = (
        (mine_group[None, None, :] == jnp.arange(groups)[:, None, None])
        & (mine_bucket[None, None, :] == jnp.arange(capacity)[None, :, None])
    ).astype(jnp.bfloat16)
    pieces = new_rows.reshape(per_region, grid_cols, slot_width, feature_width)
    outgoing = jnp.einsum(
        "gkj,jcsd->gcksd", choose, pieces, preferred_element_type=jnp.float32
    ).astype(jnp.bfloat16)
    arrived = lax.all_to_all(
        outgoing.reshape(regions, capacity, slot_width, feature_width),
        ("grp", "col"),
        split_axis=0,
        concat_axis=0,
        tiled=True,
    )
    my_slots = lax.dynamic_slice_in_dim(slot_of_agent, group_index * per_group, per_group)
    source_row = my_slots // per_region * capacity + jnp.take(bucket, my_slots)
    landed = jnp.take(
        arrived.reshape(regions * capacity, slot_width, feature_width), source_row, axis=0
    )
    tokens = lax.all_gather(landed, "col", axis=1, tiled=True)
    agents_here = cache_keys.shape[0]
    picked = tokens.reshape(lax.axis_size("row") * agents_here * slot_count, feature_width)
    query_part = jnp.dot(picked, query_weight, preferred_element_type=jnp.float32)
    key_part = jnp.dot(picked, key_weight, preferred_element_type=jnp.float32)
    value_part = jnp.dot(picked, value_weight, preferred_element_type=jnp.float32)
    summed = lax.psum_scatter(
        jnp.concatenate([query_part, key_part, value_part], axis=1)
        .reshape(lax.axis_size("row") * agents_here, slot_count, -1)
        .astype(jnp.bfloat16),
        "row",
        scatter_dimension=0,
        tiled=True,
    ).astype(jnp.float32)
    local_agents = (
        group_index * per_group + row_index * agents_here + jnp.arange(agents_here, dtype=jnp.int32)
    )
    lengths_now = jnp.take(cache_lengths, local_agents)
    counts_now = jnp.take(new_counts, local_agents)
    positions = lengths_now[:, None] + jnp.arange(slot_count, dtype=jnp.int32)[None, :]
    query_width = query_weight.shape[1]
    key_width = key_weight.shape[1]
    heads_here = query_width // HEAD_DIM
    kv_here = key_width // HEAD_DIM
    group_ratio = heads_here // kv_here
    queries = rotate_pairs(
        summed[:, :, :query_width].reshape(agents_here, slot_count, heads_here, HEAD_DIM), positions
    ).astype(jnp.bfloat16)
    fresh_keys = rotate_pairs(
        summed[:, :, query_width : query_width + key_width].reshape(
            agents_here, slot_count, kv_here, HEAD_DIM
        ),
        positions,
    ).astype(jnp.bfloat16)
    fresh_values = (
        summed[:, :, query_width + key_width :]
        .reshape(agents_here, slot_count, kv_here, HEAD_DIM)
        .astype(jnp.bfloat16)
    )
    query_rows = (
        queries.reshape(agents_here, slot_count, kv_here, group_ratio, HEAD_DIM)
        .transpose(0, 2, 3, 1, 4)
        .reshape(agents_here, kv_here, group_ratio * slot_count, HEAD_DIM)
    )
    cache_span = cache_keys.shape[1]
    stored_keys = cache_keys.reshape(agents_here, cache_span, kv_here, HEAD_DIM)
    stored_values = cache_values.reshape(agents_here, cache_span, kv_here, HEAD_DIM)
    score_scale = HEAD_DIM ** (-0.5)
    slot_of_row = jnp.arange(group_ratio * slot_count, dtype=jnp.int32) % slot_count
    fresh_index = jnp.arange(slot_count, dtype=jnp.int32)
    new_allowed = (
        (fresh_index[None, :] <= slot_of_row[:, None])[None, :, :]
        & (fresh_index[None, None, :] < counts_now[:, None, None])
    )[:, None, :, :]
    new_scores = (
        jnp.einsum("akrd,atkd->akrt", query_rows, fresh_keys, preferred_element_type=jnp.float32)
        * score_scale
    )
    cache_scores = (
        jnp.einsum("akrd,apkd->akrp", query_rows, stored_keys, preferred_element_type=jnp.float32)
        * score_scale
    )
    cache_allowed = (jnp.arange(cache_span, dtype=jnp.int32)[None, :] < lengths_now[:, None])[
        :, None, None, :
    ]
    cache_masked = jnp.where(cache_allowed, cache_scores, floor_score)
    new_masked = jnp.where(new_allowed, new_scores, floor_score)
    row_max = jnp.maximum(jnp.max(cache_masked, axis=3), jnp.max(new_masked, axis=3))
    cache_weights = jnp.where(cache_allowed, jnp.exp(cache_masked - row_max[..., None]), 0.0)
    new_weights = jnp.where(new_allowed, jnp.exp(new_masked - row_max[..., None]), 0.0)
    denominator = jnp.sum(cache_weights, axis=3) + jnp.sum(new_weights, axis=3)
    weighted = jnp.einsum(
        "akrp,apkd->akrd",
        cache_weights.astype(jnp.bfloat16),
        stored_values,
        preferred_element_type=jnp.float32,
    )
    weighted = weighted + jnp.einsum(
        "akrp,apkd->akrd",
        new_weights.astype(jnp.bfloat16),
        fresh_values,
        preferred_element_type=jnp.float32,
    )
    result = (
        (weighted / denominator[..., None])
        .reshape(agents_here, kv_here, group_ratio, slot_count, HEAD_DIM)
        .transpose(0, 3, 1, 2, 4)
        .reshape(agents_here, slot_count, query_width)
    )
    valid_slot = jnp.arange(slot_count, dtype=jnp.int32)[None, :] < counts_now[:, None]
    result = jnp.where(valid_slot[:, :, None], result, 0.0).astype(jnp.bfloat16)
    regrouped = lax.all_to_all(result, "row", split_axis=1, concat_axis=0, tiled=True)
    slot_share = slot_count // grid_rows
    choose_back = (
        jnp.arange(regions * capacity, dtype=jnp.int32)[:, None] == source_row[None, :]
    ).astype(jnp.bfloat16)
    returning = jnp.einsum(
        "qt,tsf->qsf", choose_back, regrouped, preferred_element_type=jnp.float32
    ).astype(jnp.bfloat16)
    incoming = lax.all_to_all(
        returning.reshape(regions, capacity, slot_share, query_width),
        ("grp", "col"),
        split_axis=0,
        concat_axis=0,
        tiled=True,
    ).reshape(groups, grid_cols, capacity, slot_share, query_width)
    select_back = (
        (mine_group[:, None, None] == jnp.arange(groups)[None, :, None])
        & (mine_bucket[:, None, None] == jnp.arange(capacity)[None, None, :])
    ).astype(jnp.bfloat16)
    finished = jnp.einsum(
        "jgk,gcksf->jscf", select_back, incoming, preferred_element_type=jnp.float32
    ).astype(jnp.bfloat16)
    return finished.reshape(per_region, slot_share, grid_cols * query_width)


def solution(mesh):
    placed = (
        P(("grp", "col"), None, "row"),
        P("row", "col"),
        P("row", "col"),
        P("row", "col"),
        P(("grp", "row"), None, "col"),
        P(("grp", "row"), None, "col"),
        P(),
        P(),
        P(),
    )
    return jax.shard_map(
        local, mesh=mesh, in_specs=placed, out_specs=P(("grp", "col"), "row", None), check_vma=False
    )
```

profile of v0, /device:TPU:1, one launch (start us, length us, event | category | flops | bytes accessed | tf_op | source)
XLA Modules:
  0.0 230.3 jit_solution(6798773412891268803)
XLA Ops:
  6.5 0.8 add_select_fusion
  8.1 1.2 copy.95
  10.1 1.7 copy.77
  11.8 11.6 %all-to-all-start = ((bf16[64,3,2,1024]{3,2,1,0:T(2,128)(2,1)}), bf16[64,3,2,1024]{3,2,1,0:T(2,128)(2,1)S(1)}, u32[]{:S(2)}, u32[]{:S(2)}) async-start(bf16[64,3,2,1024]{3,2,1,0:T(2,128)(2,1)} %copy.77), calls=%async_computation | async-start | bytes 1572864 | tf_op jit(solution)/shard_map/all_to_all | solution.py:72
  23.5 4.4 %sort.17 = (s32[768]{0:T(1024)}, s32[768]{0:T(1024)S(1)}) sort(s32[768]{0:T(1024)S(1)} %copy-done.7, s32[768]{0:T(1024)S(1)} %iota.103), dimensions={0}, to_apply=%region_0.1 | sort | flops 7680 | bytes 12288 | tf_op jit(solution)/shard_map/jit(argsort)/sort | solution.py:60
  27.9 1.0 gather_fusion
  29.0 17.1 %all-to-all-done = bf16[64,3,2,1024]{3,2,1,0:T(2,128)(2,1)S(1)} async-done(((bf16[64,3,2,1024]{3,2,1,0:T(2,128)(2,1)}), bf16[64,3,2,1024]{3,2,1,0:T(2,128)(2,1)S(1)}, u32[]{:S(2)}, u32[]{:S(2)}) %all-to-all-start) | async-done | bytes 786464 | tf_op jit(solution)/shard_map/all_to_all | solution.py:72
  46.2 1.4 gather_fusion.1
  49.1 33.5 %all-gather.2.cloned.1.call-done = bf16[96,16,1024]{2,0,1:T(8,128)(2,1)} async-done(((bf16[96,2,1024]{2,0,1:T(8,128)(2,1)}), bf16[96,16,1024]{2,0,1:T(8,128)(2,1)}) %all-gather.2.cloned.1.call-update) | async-done | bytes 3145744 | tf_op jit(solution)/shard_map/all_gather | solution.py:84
  82.6 3.6 %copy.79 = bf16[96,16,1024]{2,1,0:T(8,128)(2,1)S(1)} copy(bf16[96,16,1024]{2,0,1:T(8,128)(2,1)} %all-gather.2.cloned.1.call-done) | data formatting | bytes 6291456 | tf_op jit(solution)/shard_map/all_gather | solution.py:84
  86.2 3.8 %convolution_convert_fusion = bf16[1536,1024]{0,1:T(8,128)(2,1)S(1)} fusion(bf16[1536,1024]{1,0:T(8,128)(2,1)S(1)} %bitcast.78, bf16[1024,1024]{1,0:T(8,128)(2,1)S(1)} %copy-done), kind=kOutput, calls=%fused_computation.5 | convolution fusion | flops 3222798336 | bytes 8388608 | tf_op jit(solution)/shard_map/dot_general | solution.py:87
  90.1 1.2 convolution_convert_fusion.1
  91.3 1.2 convolution_convert_fusion.2
  92.5 2.1 pad_maximum_fusion
  94.5 6.3 %copy.80 = bf16[1536,1280]{1,0:T(8,128)(2,1)} copy(bf16[1536,1280]{0,1:T(8,128)(2,1)} %pad_maximum_fusion) | data formatting | bytes 7864320 | tf_op jit(solution)/shard_map/concatenate | solution.py:91
  103.5 53.5 %reduce-scatter.2.cloned.1.call-done = bf16[12,16,1280]{2,1,0:T(8,128)(2,1)} async-done(((bf16[96,16,1280]{2,1,0:T(8,128)(2,1)}), bf16[12,16,1280]{2,1,0:T(8,128)(2,1)}) %reduce-scatter.2.cloned.1.call-update) | async-done | bytes 491536 | tf_op jit(solution)/shard_map/reduce_scatter | solution.py:90
  157.0 1.1 slice.37
  161.1 1.0 fusion.1
  162.2 1.1 fusion.3
  164.6 19.8 %all_to_all.28 = bf16[12,16,1024]{2,0,1:T(8,128)(2,1)S(1)} all-to-all(bf16[12,16,1024]{2,0,1:T(8,128)(2,1)S(1)} %copy.84), channel_id=1, replica_groups=mesh['grp'=8,'row'=8,'col'=8] {'row'}, dimensions={1} | all-to-all | bytes 786432 | tf_op jit(solution)/shard_map/all_to_all | solution.py:175
  185.1 1.7 copy.88
  186.8 12.1 %all-to-all-start.2 = ((bf16[64,3,2,1024]{3,2,1,0:T(2,128)(2,1)}), bf16[64,3,2,1024]{3,2,1,0:T(2,128)(2,1)S(1)}, u32[]{:S(2)}, u32[]{:S(2)}) async-start(bf16[64,3,2,1024]{3,2,1,0:T(2,128)(2,1)} %bitcast.24), calls=%async_computation.3 | async-start | bytes 1572864 | tf_op jit(solution)/shard_map/all_to_all | solution.py:183
  199.0 22.7 %all-to-all-done.2 = bf16[64,3,2,1024]{3,2,1,0:T(2,128)(2,1)S(1)} async-done(((bf16[64,3,2,1024]{3,2,1,0:T(2,128)(2,1)}), bf16[64,3,2,1024]{3,2,1,0:T(2,128)(2,1)S(1)}, u32[]{:S(2)}, u32[]{:S(2)}) %all-to-all-start.2) | async-done | bytes 786464 | tf_op jit(solution)/shard_map/all_to_all | solution.py:183
  222.5 1.0 reshape.419
  (77 shorter events, 11.7 us)
Async XLA Ops:
  6.5 79.7 %copy-start = (bf16[1024,1024]{1,0:T(8,128)(2,1)S(1)}, bf16[1024,1024]{1,0:T(8,128)(2,1)}, u32[]{:S(2)}) copy-start(bf16[1024,1024]{1,0:T(8,128)(2,1)} %param.12) | copy-start | bytes 6291460
  9.3 14.2 %copy-start.7 = (s32[768]{0:T(1024)S(1)}, s32[768]{0:T(1024)}, u32[]{:S(2)}) copy-start(s32[768]{0:T(1024)} %param.17) | copy-start | bytes 9220
  11.8 34.4 %all-to-all-start = ((bf16[64,3,2,1024]{3,2,1,0:T(2,128)(2,1)}), bf16[64,3,2,1024]{3,2,1,0:T(2,128)(2,1)S(1)}, u32[]{:S(2)}, u32[]{:S(2)}) async-start(bf16[64,3,2,1024]{3,2,1,0:T(2,128)(2,1)} %copy.77), calls=%async_computation | async-start | bytes 1572864 | tf_op jit(solution)/shard_map/all_to_all | solution.py:72
  23.4 59.2 %all-gather.2.cloned.1.call-start = ((), (), s32[]{:S(2)}) async-start(), calls=%async_computation.4 | async-start | bytes 3538944 | tf_op jit(solution)/shard_map/all_gather | solution.py:84
  48.8 108.1 %reduce-scatter.2.cloned.1.call-start = ((), (), s32[]{:S(2)}) async-start(), calls=%async_computation.5 | async-start | bytes 4423680 | tf_op jit(solution)/shard_map/reduce_scatter | solution.py:90
  86.2 3.8 %copy-start.5 = (bf16[1024,128]{1,0:T(8,128)(2,1)S(1)}, bf16[1024,128]{1,0:T(8,128)(2,1)}, u32[]{:S(2)}) copy-start(bf16[1024,128]{1,0:T(8,128)(2,1)} %param.14) | copy-start | bytes 786436
  90.1 1.2 copy-start.6
  100.8 0.7 copy-start.1
  100.8 1.3 copy-start.2
  157.0 1.6 copy-start.3
  158.5 1.4 copy-start.4
  160.6 1.5 copy-start.8
  186.8 34.9 %all-to-all-start.2 = ((bf16[64,3,2,1024]{3,2,1,0:T(2,128)(2,1)}), bf16[64,3,2,1024]{3,2,1,0:T(2,128)(2,1)S(1)}, u32[]{:S(2)}, u32[]{:S(2)}) async-start(bf16[64,3,2,1024]{3,2,1,0:T(2,128)(2,1)} %bitcast.24), calls=%async_computation.3 | async-start | bytes 1572864 | tf_op jit(solution)/shard_map/all_to_all | solution.py:183
Sparse Core Ops, SparseCore 0:
  49.0 33.5 all-gather.1
  100.9 55.9 reduce-scatter.1
where the time goes:
time: 231 us; the launch traced here: 230 us
  waiting for transfers between devices  127 us (55%)
  local copies, waits for them, and re-layouts  24.5 us (11%)
  starting transfers between devices  24 us (10%)
  blocking collectives  19.8 us (9%)
  between operations  13.8 us (6%)
  other arithmetic  11.2 us (5%)
  matrix products  10.2 us (4%)
    reduce_scatter x1, waiting for transfers between devices, local(): lax.psum_scatter(jnp.concatenate([query_part, key_part, value_part], axis...  53.5 us
    all_gather x1, waiting for transfers between devices, local(): tokens = lax.all_gather(landed, 'col', axis=1, tiled=True)  33.5 us
    all_to_all x1, waiting for transfers between devices, local(): lax.all_to_all(returning.reshape(regions, capacity, slot_share, query_wid...  22.7 us
    all_to_all x1, blocking collectives, local(): lax.all_to_all(result, 'row', split_axis=1, concat_axis=0, tiled=True)  19.8 us
    all_to_all x1, waiting for transfers between devices, local(): lax.all_to_all(outgoing.reshape(regions, capacity, slot_width, feature_wi...  17.1 us
    all_to_all x1, starting transfers between devices, local(): lax.all_to_all(returning.reshape(regions, capacity, slot_share, query_wid...  12.1 us
    all_to_all x1, starting transfers between devices, local(): lax.all_to_all(outgoing.reshape(regions, capacity, slot_width, feature_wi...  11.6 us
    concatenate x1, local copies, waits for them, and re-layouts, local(): jnp.concatenate([query_part, key_part, value_part], axis=1)  6.26 us
  transfers between devices with their start and end apart: 4, of which 4 were waited for; matrix products, arithmetic and copies ran while one was open for 3% of the time, Pallas kernels for 0%

commit v1 on v0

v1 whole, which is shorter than its diff:
```python
import jax
import jax.numpy as jnp
import numpy as np
from jax import lax
from jax.experimental import pallas as pl
from jax.experimental.pallas import tpu as pltpu
from jax.sharding import PartitionSpec as P

HEAD_DIM = 128
SLOTS = 16
CAP = 3
rotary_base = 500000.0
floor_score = -1e30
MESH = pl.DeviceIdType.MESH

GROUPS = (8,)
N_GROUPS = len(GROUPS)
N_ROW = 8
PLUS, MINUS = 0, 1
MESSAGES = ((1, 4), (0, 3), (1, 3), (0, 2), (1, 2), (0, 1), (1, 1))
OFFSETS = (4, 3, -3, 2, -2, 1, -1, 0)


def group_columns():
    found, at = [], 0
    for i, heads in enumerate(GROUPS):
        width = (heads + (2 if i == 0 else 0)) * HEAD_DIM
        found.append((at, width // 2))
        at += width
    return found


COLUMNS = group_columns()


def message_index(direction, half, distance):
    long = 1 if half == direction else 0
    return MESSAGES.index((long, distance))


def whole_wait(ref, sem):
    pltpu.make_async_copy(ref, ref, sem).wait()


def kernel(*refs):
    refs = list(refs)
    take = lambda n: [refs.pop(0) for _ in range(n)]
    idx, cosine, sine, rows, wq, wk, wv, keys, values = take(9)
    (out,) = take(1)
    outg, arrv, xg, wbuf, kbuf, vbuf, kn, vn = take(8)
    sbuf = [take(2) for _ in range(N_GROUPS)]
    rbuf = [take(2) for _ in range(N_GROUPS)]
    qs, zs, zr, bo, inc = (take(N_GROUPS) for _ in range(5))
    local_sem, d_send, d_recv, ag_send, ag_recv, rs_send, rs_recv, z_send, z_recv, b_send, b_recv = take(11)

    g = lax.axis_index("grp")
    r = lax.axis_index("row")
    c = lax.axis_index("col")
    me = g * 8 + c
    SEND, RECV, BACK, FING, FINK, LENS, CNTS = 0, 24, 120, 312, 324, 336, 348

    loads = [
        pltpu.make_async_copy(wk, wbuf.at[:, pl.ds(0, HEAD_DIM)], local_sem.at[0]),
        pltpu.make_async_copy(wv, wbuf.at[:, pl.ds(HEAD_DIM, HEAD_DIM)], local_sem.at[1]),
        pltpu.make_async_copy(wq, wbuf.at[:, pl.ds(2 * HEAD_DIM, 1024)], local_sem.at[2]),
        pltpu.make_async_copy(keys, kbuf, local_sem.at[3]),
        pltpu.make_async_copy(values, vbuf, local_sem.at[4]),
    ]
    for load in loads:
        load.start()

    barrier = pltpu.get_barrier_semaphore()
    for i in range(8):
        for o in range(8):
            if (i, o) != (0, 0):
                pl.semaphore_signal(
                    barrier, inc=1, device_id=(lax.rem(g + i, 8), r, lax.rem(c + o, 8)), device_id_type=MESH
                )
    for i in range(1, 8):
        pl.semaphore_signal(barrier, inc=1, device_id=(g, lax.rem(r + i, 8), c), device_id_type=MESH)

    def fill(target_group):
        for k in range(CAP):
            j = idx[0, SEND + target_group * CAP + k]
            row = rows[j]
            for cc in range(8):
                outg[target_group * 8 + cc, k] = row[:, cc * 128 : (cc + 1) * 128]

    order = (4, 3, 5, 2, 6, 1, 7, 0)
    fill(lax.rem(g + order[0], 8))
    pl.semaphore_wait(barrier, 70)

    for n, i in enumerate(order):
        tg = lax.rem(g + i, 8)
        if n:
            fill(tg)
        for o in range(8):
            tc = lax.rem(c + o, 8)
            if (i, o) == (0, 0):
                arrv[me] = outg[me]
                continue
            pltpu.make_async_remote_copy(
                src_ref=outg.at[tg * 8 + tc],
                dst_ref=arrv.at[me],
                send_sem=d_send,
                recv_sem=d_recv,
                device_id=(tg, r, tc),
                device_id_type=MESH,
            ).start()
    whole_wait(arrv.at[pl.ds(0, 63)], d_recv)

    x, p = lax.div(c, 2), lax.rem(c, 2)
    ahead = lax.rem(x + 1 + 2 * p, 4) * 2 + p
    behind = lax.rem(x + 3 + 2 * p, 4) * 2 + p
    far = lax.rem(x + 2, 4) * 2 + p
    sibling = c + 1 - 2 * p
    block_of = [lax.rem(r + o + 8, 8) for o in OFFSETS]

    def ag_copy(t, origin, target, kind):
        k = block_of[t]
        return pltpu.make_async_remote_copy(
            src_ref=xg.at[k, origin],
            dst_ref=xg.at[k, origin],
            send_sem=ag_send,
            recv_sem=ag_recv.at[t, kind],
            device_id=(g, r, target),
            device_id_type=MESH,
        )

    def ag_wait(t, kind):
        whole_wait(xg.at[block_of[t], c], ag_recv.at[t, kind])

    def ag_start(t):
        k = block_of[t]
        for a in range(12):
            xg[k, c, a] = arrv[lax.div(idx[0, RECV + k * 12 + a], CAP), lax.rem(idx[0, RECV + k * 12 + a], CAP)]
        ag_copy(t, c, ahead, 1).start()
        ag_copy(t, c, behind, 2).start()
        ag_copy(t, c, sibling, 0).start()

    def ag_first(t):
        ag_wait(t, 1)
        ag_copy(t, behind, ahead, 3).start()
        ag_copy(t, behind, sibling, 4).start()
        ag_wait(t, 2)
        ag_copy(t, ahead, sibling, 5).start()

    def ag_second(t):
        ag_wait(t, 3)
        ag_copy(t, far, sibling, 6).start()

    def ag_finish(t):
        for kind in (0, 4, 5, 6):
            ag_wait(t, kind)

    def tokens(t):
        k = block_of[t]
        return jnp.concatenate([xg[k, cc].reshape(12 * SLOTS, 128) for cc in range(8)], axis=1)

    up, down = lax.rem(r + 1, 8), lax.rem(r + 7, 8)
    toward = (up, down)

    def columns(gi, half):
        first, width = COLUMNS[gi]
        return pl.ds(first + half * width, width)

    def partial(gi, half, t):
        return jnp.dot(tokens(t), wbuf[:, columns(gi, half)], preferred_element_type=jnp.float32)

    def rs_wait(gi, direction, m):
        whole_wait(rbuf[gi][direction].at[m], rs_recv.at[gi, direction, m])

    def rs_step(gi, m):
        is_long, distance = MESSAGES[m]
        for direction in (PLUS, MINUS):
            half = direction if is_long else 1 - direction
            t = OFFSETS.index(distance if direction == PLUS or distance == 4 else -distance)
            part = partial(gi, half, t)
            if (is_long, distance + 1) in MESSAGES:
                before = MESSAGES.index((is_long, distance + 1))
                rs_wait(gi, direction, before)
                part = part + rbuf[gi][direction][before].astype(jnp.float32)
            sbuf[gi][direction][m] = part.astype(jnp.bfloat16)
            pltpu.make_async_remote_copy(
                src_ref=sbuf[gi][direction].at[m],
                dst_ref=rbuf[gi][direction].at[m],
                send_sem=rs_send.at[gi, direction],
                recv_sem=rs_recv.at[gi, direction, m],
                device_id=(g, toward[direction], c),
                device_id_type=MESH,
            ).start()

    def rotate(u):
        return u * cosine[...] + pltpu.roll(u, 64, 1) * sine[...]

    def finish(gi):
        start = 0
        for half in (0, 1):
            own = partial(gi, half, 7)
            for direction in (PLUS, MINUS):
                m = message_index(direction, half, 1)
                rs_wait(gi, direction, m)
                own = own + rbuf[gi][direction][m].astype(jnp.float32)
            for b in range(COLUMNS[gi][1] // 128):
                piece = own[:, b * 128 : (b + 1) * 128]
                at = start + b - (2 if gi == 0 else 0)
                if at == -2:
                    kn[...] = rotate(piece).astype(jnp.bfloat16).reshape(12, SLOTS, 128)
                elif at == -1:
                    vn[...] = piece.astype(jnp.bfloat16).reshape(12, SLOTS, 128)
                else:
                    qs[gi][:, at] = rotate(piece).astype(jnp.bfloat16).reshape(12, SLOTS, 128)
            start += COLUMNS[gi][1] // 128

    def attend(gi):
        heads = GROUPS[gi]
        n = heads * SLOTS
        scale = HEAD_DIM ** (-0.5) * float(np.log2(np.e))
        row_s = lax.broadcasted_iota(jnp.int32, (n, SLOTS), 0) % SLOTS
        col_t = lax.broadcasted_iota(jnp.int32, (n, SLOTS), 1)
        causal = col_t <= row_s
        place = lax.broadcasted_iota(jnp.int32, (n, 512), 1)
        slot = lax.broadcasted_iota(jnp.int32, (n, 128), 0) % SLOTS
        i = lax.broadcasted_iota(jnp.int32, (n, n), 0)
        j = lax.broadcasted_iota(jnp.int32, (n, n), 1)
        swap = ((i % heads) * SLOTS + i // heads == j).astype(jnp.float32).astype(jnp.bfloat16)
        last = (((1,), (1,)), ((), ()))

        def one(a, _):
            length, count = idx[0, LENS + a], idx[0, CNTS + a]
            q = qs[gi][a].reshape(n, 128)
            s1 = lax.dot_general(q, kbuf[a], last, preferred_element_type=jnp.float32) * scale
            s2 = lax.dot_general(q, kn[a], last, preferred_element_type=jnp.float32) * scale
            s1 = jnp.where(place < length, s1, floor_score)
            s2 = jnp.where(causal & (col_t < count), s2, floor_score)
            top = jnp.maximum(jnp.max(s1, axis=1, keepdims=True), jnp.max(s2, axis=1, keepdims=True))
            p1, p2 = jnp.exp2(s1 - top), jnp.exp2(s2 - top)
            den = jnp.sum(p1, axis=1, keepdims=True) + jnp.sum(p2, axis=1, keepdims=True)
            mixed = jnp.dot(p1.astype(jnp.bfloat16), vbuf[a], preferred_element_type=jnp.float32)
            mixed = mixed + jnp.dot(p2.astype(jnp.bfloat16), vn[a], preferred_element_type=jnp.float32)
            mixed = jnp.where(slot < count, mixed / den, 0.0).astype(jnp.bfloat16)
            swapped = jnp.dot(swap, mixed, preferred_element_type=jnp.float32).astype(jnp.bfloat16)
            zs[gi][:, a] = swapped.reshape(8, 2 * heads, 128)
            return 0

        lax.fori_loop(0, 12, one, 0, unroll=2)

    def z_start(gi):
        for i in (4, 3, 5, 2, 6, 1, 7):
            other = lax.rem(r + i, 8)
            pltpu.make_async_remote_copy(
                src_ref=zs[gi].at[other],
                dst_ref=zr[gi].at[r],
                send_sem=z_send.at[gi],
                recv_sem=z_recv.at[gi],
                device_id=(g, other, c),
                device_id_type=MESH,
            ).start()
        zr[gi][r] = zs[gi][r]

    def back_start(gi):
        whole_wait(zr[gi].at[pl.ds(0, 7)], z_recv.at[gi])
        for i in order:
            tg = lax.rem(g + i, 8)
            for o in range(8):
                tc = lax.rem(c + o, 8)
                target = tg * 8 + tc
                for k in range(CAP):
                    a = idx[0, BACK + target * CAP + k]
                    bo[gi][target, k] = zr[gi][lax.div(a, 12), lax.rem(a, 12)]
                if (i, o) == (0, 0):
                    inc[gi][g, c] = bo[gi][target]
                    continue
                pltpu.make_async_remote_copy(
                    src_ref=bo[gi].at[target],
                    dst_ref=inc[gi].at[g, c],
                    send_sem=b_send.at[gi],
                    recv_sem=b_recv.at[gi],
                    device_id=(tg, r, tc),
                    device_id_type=MESH,
                ).start()

    def back_finish(gi):
        whole_wait(bo[gi].at[pl.ds(0, 63)], b_recv.at[gi])
        for j in range(12):
            out[j, :, gi] = inc[gi][idx[0, FING + j], :, idx[0, FINK + j]]

    for t in (0, 1, 2):
        ag_start(t)
    ag_first(0)
    for t in (3, 4):
        ag_start(t)
    ag_second(0)
    ag_first(1)
    ag_first(2)
    for t in (5, 6, 7):
        ag_start(t)
    for load in loads[:3]:
        load.wait()
    ag_finish(0)
    rs_step(0, 0)
    for t in (1, 2):
        ag_second(t)
    for t in (3, 4):
        ag_first(t)
    for t in (1, 2):
        ag_finish(t)
    rs_step(0, 1)
    for t in (3, 4):
        ag_second(t)
    for t in (5, 6, 7):
        ag_first(t)
    rs_step(0, 2)
    for t in (5, 6, 7):
        ag_second(t)
    for t in (3, 4):
        ag_finish(t)
    rs_step(0, 3)
    for t in (5, 6, 7):
        ag_finish(t)
    for m in (4, 5, 6):
        rs_step(0, m)
    for load in loads[3:]:
        load.wait()

    if N_GROUPS == 1:
        finish(0)
        attend(0)
        z_start(0)
        back_start(0)
        back_finish(0)
    else:
        rs_step(1, 0)
        rs_step(1, 1)
        finish(0)
        rs_step(1, 2)
        attend(0)
        z_start(0)
        rs_step(1, 3)
        rs_step(1, 4)
        back_start(0)
        rs_step(1, 5)
        rs_step(1, 6)
        finish(1)
        attend(1)
        z_start(1)
        back_finish(0)
        back_start(1)
        back_finish(1)

    whole_wait(outg.at[pl.ds(0, 63)], d_send)
    whole_wait(xg.at[pl.ds(0, 7)], ag_send)
    for gi in range(N_GROUPS):
        for direction in (PLUS, MINUS):
            whole_wait(sbuf[gi][direction], rs_send.at[gi, direction])
        whole_wait(zs[gi].at[pl.ds(0, 7)], z_send.at[gi])
        whole_wait(bo[gi].at[pl.ds(0, 63)], b_send.at[gi])


def local(
    new_rows,
    query_weight,
    key_weight,
    value_weight,
    cache_keys,
    cache_values,
    region_agents,
    new_counts,
    cache_lengths,
):
    g = lax.axis_index("grp")
    r = lax.axis_index("row")
    c = lax.axis_index("col")
    per_group = 96
    ra = region_agents.reshape(64, 12)
    earlier = jnp.arange(12)[:, None] > jnp.arange(12)[None, :]
    three = jnp.arange(CAP, dtype=jnp.int32)
    mine = lax.dynamic_slice_in_dim(region_agents, (g * 8 + c) * 12, 12) // per_group
    mine_bucket = jnp.sum(((mine[:, None] == mine[None, :]) & earlier).astype(jnp.int32), axis=1)
    pick = (mine[:, None, None] == jnp.arange(8, dtype=jnp.int32)[None, :, None]) & (
        mine_bucket[:, None, None] == three[None, None, :]
    )
    send = jnp.sum(jnp.where(pick, jnp.arange(12, dtype=jnp.int32)[:, None, None], 0), axis=0).reshape(24)
    here = ra // per_group == g
    bucket = jnp.sum((here[:, None, :] & earlier[None]).astype(jnp.int32), axis=2)
    number = jnp.where(here, ra - g * per_group, -1)
    back = jnp.sum(
        jnp.where(here[:, :, None] & (bucket[:, :, None] == three[None, None, :]), number[:, :, None], 0), axis=1
    ).reshape(192)
    place = jnp.arange(64, dtype=jnp.int32)[:, None] * CAP + bucket
    recv = jnp.sum(
        jnp.where(
            number.reshape(1, 768) == jnp.arange(per_group, dtype=jnp.int32)[:, None], place.reshape(1, 768), 0
        ),
        axis=1,
    )
    first = g * per_group + r * 12
    lengths = lax.dynamic_slice_in_dim(cache_lengths, first, 12)
    counts = lax.dynamic_slice_in_dim(new_counts, first, 12)
    table = jnp.concatenate([send, recv, back, mine, mine_bucket, lengths, counts]).reshape(1, 360)

    positions = (lengths[:, None] + jnp.arange(SLOTS, dtype=jnp.int32)[None, :]).astype(jnp.float32)
    exponent = jnp.arange(64, dtype=jnp.float32) * (2.0 / HEAD_DIM)
    angles = positions.reshape(192, 1) * (rotary_base ** (-exponent))
    cosine, sine = jnp.cos(angles), jnp.sin(angles)
    cosine = jnp.concatenate([cosine, cosine], axis=1)
    sine = jnp.concatenate([-sine, sine], axis=1)

    bf, vmem = jnp.bfloat16, pltpu.VMEM
    scratch = [
        vmem((64, CAP, SLOTS, 128), bf),
        vmem((64, CAP, SLOTS, 128), bf),
        vmem((8, 8, 12, SLOTS, 128), bf),
        vmem((1024, 1280), bf),
        vmem((12, 512, 128), bf),
        vmem((12, 512, 128), bf),
        vmem((12, SLOTS, 128), bf),
        vmem((12, SLOTS, 128), bf),
    ]
    for _ in range(2):
        for gi in range(N_GROUPS):
            scratch += [vmem((7, 192, COLUMNS[gi][1]), bf)] * 2
    scratch += [vmem((12, h, SLOTS, 128), bf) for h in GROUPS]
    scratch += [vmem((8, 12, 2 * h, 128), bf) for h in GROUPS] * 2
    scratch += [vmem((64, CAP, 2 * h, 128), bf) for h in GROUPS]
    scratch += [vmem((8, 8, CAP, 2 * h, 128), bf) for h in GROUPS]
    dma = pltpu.SemaphoreType.DMA
    scratch += [
        dma((5,)),
        dma(()),
        dma(()),
        dma(()),
        dma((8, 7)),
        dma((N_GROUPS, 2)),
        dma((N_GROUPS, 2, 7)),
        dma((N_GROUPS,)),
        dma((N_GROUPS,)),
        dma((N_GROUPS,)),
        dma((N_GROUPS,)),
    ]
    in_vmem = pl.BlockSpec(memory_space=pltpu.VMEM)
    anywhere = pl.BlockSpec(memory_space=pl.ANY)
    heads = GROUPS[0]
    result = pl.pallas_call(
        kernel,
        out_shape=jax.ShapeDtypeStruct((12, 8, N_GROUPS, 2 * heads, 128), bf),
        in_specs=[pl.BlockSpec(memory_space=pltpu.SMEM)] + [in_vmem] * 3 + [anywhere] * 5,
        out_specs=in_vmem,
        scratch_shapes=scratch,
        compiler_params=pltpu.CompilerParams(
            collective_id=0, has_side_effects=True, vmem_limit_bytes=56 * 2**20
        ),
    )(table, cosine, sine, new_rows, query_weight, key_weight, value_weight, cache_keys, cache_values)
    return (
        result.reshape(12, 8, N_GROUPS, 2, heads, 128).transpose(0, 3, 1, 2, 4, 5).reshape(12, 2, 8192)
    )


def solution(mesh):
    placed = (
        P(("grp", "col"), None, "row"),
        P("row", "col"),
        P("row", "col"),
        P("row", "col"),
        P(("grp", "row"), None, "col"),
        P(("grp", "row"), None, "col"),
        P(),
        P(),
        P(),
    )
    return jax.shard_map(
        local, mesh=mesh, in_specs=placed, out_specs=P(("grp", "col"), "row", None), check_vma=False
    )
```

time: 231 us -> 135 us (0.58)
  waiting for transfers between devices: 127 us -> 0 us
  Pallas kernels: 0 us -> 125 us
  starting transfers between devices: 24 us -> 0 us
  blocking collectives: 19.8 us -> 0 us
  local copies, waits for them, and re-layouts: 24.5 us -> 5.25 us
  between operations: 13.8 us -> 0.1 us
  matrix products: 10.2 us -> 0 us
  other arithmetic: 11.2 us -> 3.42 us
    pallas_call x0 -> x1, Pallas kernels: none -> 125 us  [local(): pl.pallas_call(kernel, out_shape=jax.ShapeDtypeStruct((12, 8, N_GROUPS, 2...]
    reduce_scatter x1 -> x0, waiting for transfers between devices: 53.5 us -> none  [local(): lax.psum_scatter(jnp.concatenate([query_part, key_part, value_part], axis...]
    all_to_all x2 -> x0, waiting for transfers between devices: 39.9 us -> none  [the longest x1 22.7 us: local(): lax.all_to_all(returning.reshape(regions, capacity, slot_share, query_wid...]
    all_gather x1 -> x0, waiting for transfers between devices: 33.5 us -> none  [local(): tokens = lax.all_gather(landed, 'col', axis=1, tiled=True)]
    all_to_all x2 -> x0, starting transfers between devices: 23.7 us -> none  [the longest x1 12.1 us: local(): lax.all_to_all(returning.reshape(regions, capacity, slot_share, query_wid...]
    all_to_all x1 -> x0, blocking collectives: 19.8 us -> none  [local(): lax.all_to_all(result, 'row', split_axis=1, concat_axis=0, tiled=True)]
    dot_general x10 -> x0, matrix products: 10.2 us -> none  [the longest x1 3.82 us: local(): jnp.dot(picked, query_weight, preferred_element_type=jnp.float32)]
    concatenate x1, local copies, waits for them, and re-layouts: 6.26 us -> 0.08 us  [local(): jnp.concatenate([send, recv, back, mine, mine_bucket, lengths, counts])]
  transfers between devices with their start and end apart: 4 -> 0, of which waited for: 4 -> 0; matrix products, arithmetic and copies ran while one was open for 3% -> 0% of each run, Pallas kernels for 0% -> 0%
where the time goes in v1:
time: 135 us; the launch traced here: 134 us
  Pallas kernels  125 us (93%)
  local copies, waits for them, and re-layouts  5.25 us (4%)
  other arithmetic  3.42 us (3%)
    pallas_call x1, Pallas kernels, local(): pl.pallas_call(kernel, out_shape=jax.ShapeDtypeStruct((12, 8, N_GROUPS, 2...  125 us

profile of v1, /device:TPU:1, one launch (start us, length us, event | category | flops | bytes accessed | tf_op | source)
XLA Modules:
  0.0 134.3 jit_solution(17638587944624740012)
XLA Ops:
  0.0 0.8 and_select_fusion
  0.8 0.8 dynamic_slice.10
  1.5 0.8 dynamic_slice.11
  2.3 0.2 convert_reduce_fusion.1
  2.5 0.1 select_reduce_fusion.2
  2.7 0.1 copy.12
  3.0 0.7 fusion.5
  3.7 0.1 and.70
  3.8 0.1 sub.32
  3.9 0.1 div.30
  4.1 0.1 copy.13
  4.2 0.1 convert_reduce_fusion
  4.4 0.1 copy.14
  4.5 0.1 add.65
  4.6 0.1 select_reduce_fusion
  4.7 0.1 copy.17
  4.8 0.1 reshape.196
  4.9 0.1 concatenate.9
  5.0 0.6 reshape.197.refs_0_
  5.6 0.4 fusion.1
  6.0 0.8 pad_maximum_fusion
  6.8 125.5 %shard_map.91 = bf16[12,8,1,16,128]{4,3,2,1,0:T(8,128)(2,1)} custom-call(s32[1,360]{1,0:T(1,128)} %reshape.197.refs_0_, f32[192,128]{1,0:T(8,128)} %get-tuple-element.14.refs_1_, f32[192,128]{1,0:T(8,128)} %get-tuple-element.15.refs_2_, bf16[12,16,1024]{2,1,0:T(8,128)(2,1)} %refs_3_.1, bf16[1024,1024]{1,0:T(8,128)(2,1)} %refs_4_.1, ...), custom_call_target="tpu_custom_call" | custom-call | tf_op jit(solution)/shard_map/pallas_call | solution.py:444
  132.3 1.1 copy.18
  133.4 0.8 reshape.199
  (12 shorter events, 0.4 us)

commit v2 on v1

--- a/solution.py
+++ b/solution.py
@@ -12,8 +12,9 @@
 rotary_base = 500000.0
 floor_score = -1e30
 MESH = pl.DeviceIdType.MESH
-
-GROUPS = (8,)
+SEND, RECV, BACK, SEAT, LENS, CNTS, TABLE = 0, 24, 120, 312, 328, 344, 360
+
+GROUPS = (4, 4)
 N_GROUPS = len(GROUPS)
 N_ROW = 8
 PLUS, MINUS = 0, 1
@@ -45,8 +46,9 @@
 def kernel(*refs):
     refs = list(refs)
     take = lambda n: [refs.pop(0) for _ in range(n)]
-    idx, cosine, sine, rows, wq, wk, wv, keys, values = take(9)
+    agents, all_counts, all_lengths, frequency, rows, wq, wk, wv, keys, values = take(10)
     (out,) = take(1)
+    table, idx, cosine, sine = take(4)
     outg, arrv, xg, wbuf, kbuf, vbuf, kn, vn = take(8)
     sbuf = [take(2) for _ in range(N_GROUPS)]
     rbuf = [take(2) for _ in range(N_GROUPS)]
@@ -57,7 +59,6 @@
     r = lax.axis_index("row")
     c = lax.axis_index("col")
     me = g * 8 + c
-    SEND, RECV, BACK, FING, FINK, LENS, CNTS = 0, 24, 120, 312, 324, 336, 348
 
     loads = [
         pltpu.make_async_copy(wk, wbuf.at[:, pl.ds(0, HEAD_DIM)], local_sem.at[0]),
@@ -79,9 +80,37 @@
     for i in range(1, 8):
         pl.semaphore_signal(barrier, inc=1, device_id=(g, lax.rem(r + i, 8), c), device_id_type=MESH)
 
+    ra = agents[...]
+    flat = lax.broadcasted_iota(jnp.int32, (1, 768), 1)
+    region = lax.shift_right_logical(flat * 5462, 16)
+    within = flat - region * 12
+    served = lax.shift_right_logical(ra * 683, 16)
+    bucket = jnp.zeros((1, 768), jnp.int32)
+    for d in range(1, 12):
+        same = (pltpu.roll(served, d, 1) == served) & (within >= d)
+        bucket = bucket + same.astype(jnp.int32)
+    place = region * CAP + bucket
+    seat = served * CAP + bucket
+
+    def pick(count, chosen, offset, values, most):
+        want = lax.broadcasted_iota(jnp.int32, (count, 768), 0) + offset
+        hit = jnp.broadcast_to(chosen, (count, 768)) == want
+        total = jnp.sum(jnp.where(hit, jnp.broadcast_to(values, (count, 768)), 0), axis=1, keepdims=True)
+        return jnp.broadcast_to(jnp.clip(total, 0, most), (count, 128))
+
+    table[SEND : SEND + 24] = pick(24, jnp.where(region == me, seat, -1), 0, within, 11)
+    table[RECV : RECV + 96] = pick(96, ra, g * 96, place, 64 * CAP - 1)
+    table[BACK : BACK + 192] = pick(192, jnp.where(served == g, place, -1), 0, ra - g * 96, 95)
+    table[SEAT : SEAT + 16] = pick(16, flat, me * 12, seat, 8 * CAP - 1)
+    table[LENS : LENS + 16] = pick(16, flat, g * 96 + r * 12, all_lengths[...], 512)
+    table[CNTS : CNTS + 16] = pick(16, flat, g * 96 + r * 12, all_counts[...], SLOTS)
+    to_scalars = pltpu.make_async_copy(table, idx, local_sem.at[5])
+    to_scalars.start()
+    to_scalars.wait()
+
     def fill(target_group):
         for k in range(CAP):
-            j = idx[0, SEND + target_group * CAP + k]
+            j = idx[SEND + target_group * CAP + k, 0]
             row = rows[j]
             for cc in range(8):
                 outg[target_group * 8 + cc, k] = row[:, cc * 128 : (cc + 1) * 128]
@@ -107,6 +136,14 @@
                 device_id=(tg, r, tc),
                 device_id_type=MESH,
             ).start()
+
+    slots = lax.broadcasted_iota(jnp.int32, (SLOTS, 128), 0)
+    lanes = lax.broadcasted_iota(jnp.int32, (SLOTS, 128), 1)
+    for a in range(12):
+        angle = (slots + idx[LENS + a, 0]).astype(jnp.float32) * frequency[...]
+        cosine[a * SLOTS : (a + 1) * SLOTS] = jnp.cos(angle)
+        turn = jnp.sin(angle)
+        sine[a * SLOTS : (a + 1) * SLOTS] = jnp.where(lanes < 64, -turn, turn)
     whole_wait(arrv.at[pl.ds(0, 63)], d_recv)
 
     x, p = lax.div(c, 2), lax.rem(c, 2)
@@ -133,7 +170,7 @@
     def ag_start(t):
         k = block_of[t]
         for a in range(12):
-            xg[k, c, a] = arrv[lax.div(idx[0, RECV + k * 12 + a], CAP), lax.rem(idx[0, RECV + k * 12 + a], CAP)]
+            xg[k, c, a] = arrv[lax.div(idx[RECV + k * 12 + a, 0], CAP), lax.rem(idx[RECV + k * 12 + a, 0], CAP)]
         ag_copy(t, c, ahead, 1).start()
         ag_copy(t, c, behind, 2).start()
         ag_copy(t, c, sibling, 0).start()
@@ -227,7 +264,7 @@
         last = (((1,), (1,)), ((), ()))
 
         def one(a, _):
-            length, count = idx[0, LENS + a], idx[0, CNTS + a]
+            length, count = idx[LENS + a, 0], idx[CNTS + a, 0]
             q = qs[gi][a].reshape(n, 128)
             s1 = lax.dot_general(q, kbuf[a], last, preferred_element_type=jnp.float32) * scale
             s2 = lax.dot_general(q, kn[a], last, preferred_element_type=jnp.float32) * scale
@@ -266,7 +303,7 @@
                 tc = lax.rem(c + o, 8)
                 target = tg * 8 + tc
                 for k in range(CAP):
-                    a = idx[0, BACK + target * CAP + k]
+                    a = idx[BACK + target * CAP + k, 0]
                     bo[gi][target, k] = zr[gi][lax.div(a, 12), lax.rem(a, 12)]
                 if (i, o) == (0, 0):
                     inc[gi][g, c] = bo[gi][target]
@@ -283,7 +320,8 @@
     def back_finish(gi):
         whole_wait(bo[gi].at[pl.ds(0, 63)], b_recv.at[gi])
         for j in range(12):
-            out[j, :, gi] = inc[gi][idx[0, FING + j], :, idx[0, FINK + j]]
+            seat_j = idx[SEAT + j, 0]
+            out[j, :, gi] = inc[gi][lax.div(seat_j, CAP), :, lax.rem(seat_j, CAP)]
 
     for t in (0, 1, 2):
         ag_start(t)
@@ -368,46 +406,14 @@
     new_counts,
     cache_lengths,
 ):
-    g = lax.axis_index("grp")
-    r = lax.axis_index("row")
-    c = lax.axis_index("col")
-    per_group = 96
-    ra = region_agents.reshape(64, 12)
-    earlier = jnp.arange(12)[:, None] > jnp.arange(12)[None, :]
-    three = jnp.arange(CAP, dtype=jnp.int32)
-    mine = lax.dynamic_slice_in_dim(region_agents, (g * 8 + c) * 12, 12) // per_group
-    mine_bucket = jnp.sum(((mine[:, None] == mine[None, :]) & earlier).astype(jnp.int32), axis=1)
-    pick = (mine[:, None, None] == jnp.arange(8, dtype=jnp.int32)[None, :, None]) & (
-        mine_bucket[:, None, None] == three[None, None, :]
-    )
-    send = jnp.sum(jnp.where(pick, jnp.arange(12, dtype=jnp.int32)[:, None, None], 0), axis=0).reshape(24)
-    here = ra // per_group == g
-    bucket = jnp.sum((here[:, None, :] & earlier[None]).astype(jnp.int32), axis=2)
-    number = jnp.where(here, ra - g * per_group, -1)
-    back = jnp.sum(
-        jnp.where(here[:, :, None] & (bucket[:, :, None] == three[None, None, :]), number[:, :, None], 0), axis=1
-    ).reshape(192)
-    place = jnp.arange(64, dtype=jnp.int32)[:, None] * CAP + bucket
-    recv = jnp.sum(
-        jnp.where(
-            number.reshape(1, 768) == jnp.arange(per_group, dtype=jnp.int32)[:, None], place.reshape(1, 768), 0
-        ),
-        axis=1,
-    )
-    first = g * per_group + r * 12
-    lengths = lax.dynamic_slice_in_dim(cache_lengths, first, 12)
-    counts = lax.dynamic_slice_in_dim(new_counts, first, 12)
-    table = jnp.concatenate([send, recv, back, mine, mine_bucket, lengths, counts]).reshape(1, 360)
-
-    positions = (lengths[:, None] + jnp.arange(SLOTS, dtype=jnp.int32)[None, :]).astype(jnp.float32)
-    exponent = jnp.arange(64, dtype=jnp.float32) * (2.0 / HEAD_DIM)
-    angles = positions.reshape(192, 1) * (rotary_base ** (-exponent))
-    cosine, sine = jnp.cos(angles), jnp.sin(angles)
-    cosine = jnp.concatenate([cosine, cosine], axis=1)
-    sine = jnp.concatenate([-sine, sine], axis=1)
-
+    half_frequency = rotary_base ** (-np.arange(64) * (2.0 / HEAD_DIM))
+    frequency = jnp.asarray(np.tile(half_frequency, 2).astype(np.float32).reshape(1, 128))
     bf, vmem = jnp.bfloat16, pltpu.VMEM
     scratch = [
+        vmem((TABLE, 128), jnp.int32),
+        pltpu.SMEM((TABLE, 128), jnp.int32),
+        vmem((192, 128), jnp.float32),
+        vmem((192, 128), jnp.float32),
         vmem((64, CAP, SLOTS, 128), bf),
         vmem((64, CAP, SLOTS, 128), bf),
         vmem((8, 8, 12, SLOTS, 128), bf),
@@ -426,7 +432,7 @@
     scratch += [vmem((8, 8, CAP, 2 * h, 128), bf) for h in GROUPS]
     dma = pltpu.SemaphoreType.DMA
     scratch += [
-        dma((5,)),
+        dma((6,)),
         dma(()),
         dma(()),
         dma(()),
@@ -444,13 +450,24 @@
     result = pl.pallas_call(
         kernel,
         out_shape=jax.ShapeDtypeStruct((12, 8, N_GROUPS, 2 * heads, 128), bf),
-        in_specs=[pl.BlockSpec(memory_space=pltpu.SMEM)] + [in_vmem] * 3 + [anywhere] * 5,
+        in_specs=[in_vmem] * 5 + [anywhere] * 5,
         out_specs=in_vmem,
         scratch_shapes=scratch,
         compiler_params=pltpu.CompilerParams(
             collective_id=0, has_side_effects=True, vmem_limit_bytes=56 * 2**20
         ),
-    )(table, cosine, sine, new_rows, query_weight, key_weight, value_weight, cache_keys, cache_values)
+    )(
+        region_agents.reshape(1, 768),
+        new_counts.reshape(1, 768),
+        cache_lengths.reshape(1, 768),
+        frequency,
+        new_rows,
+        query_weight,
+        key_weight,
+        value_weight,
+        cache_keys,
+        cache_values,
+    )
     return (
         result.reshape(12, 8, N_GROUPS, 2, heads, 128).transpose(0, 3, 1, 2, 4, 5).reshape(12, 2, 8192)
     )

time: 135 us -> 125 us (0.926)
  Pallas kernels: 125 us -> 118 us
  other arithmetic: 3.42 us -> 0 us
    pallas_call x1, Pallas kernels: 125 us -> 118 us  [local(): pl.pallas_call(kernel, out_shape=jax.ShapeDtypeStruct((12, 8, N_GROUPS, 2...]
    reshape x3, local copies, waits for them, and re-layouts: 0.81 us -> 3.81 us  [the longest x1 1.28 us: local(): cache_lengths.reshape(1, 768)]
    dynamic_slice x2 -> x0, local copies, waits for them, and re-layouts: 1.52 us -> none  [the longest x1 0.76 us: local(): lengths = lax.dynamic_slice_in_dim(cache_lengths, first, 12)]
    select_n x3 -> x0, other arithmetic: 1.49 us -> none  [the longest x1 0.77 us: local(): lax.dynamic_slice_in_dim(region_agents, (g * 8 + c) * 12, 12) // per_group]
where the time goes in v2:
time: 125 us; the launch traced here: 124 us
  Pallas kernels  118 us (94%)
  local copies, waits for them, and re-layouts  5.84 us (5%)
    pallas_call x1, Pallas kernels, local(): pl.pallas_call(kernel, out_shape=jax.ShapeDtypeStruct((12, 8, N_GROUPS, 2...  118 us

profile of v2, /device:TPU:1, one launch (start us, length us, event | category | flops | bytes accessed | tf_op | source)
XLA Modules:
  0.0 124.4 jit_solution(3796143626868147897)
XLA Ops:
  0.0 1.3 %reshape.15.refs_0_ = s32[1,768]{1,0:T(1,128)} reshape(s32[768]{0:T(1024)} %param.16) | data formatting | bytes 6144 | tf_op jit(solution)/shard_map/reshape | solution.py:460
  1.3 1.3 %reshape.16.refs_1_ = s32[1,768]{1,0:T(1,128)} reshape(s32[768]{0:T(1024)} %param.17) | data formatting | bytes 6144 | tf_op jit(solution)/shard_map/reshape | solution.py:461
  2.5 1.3 %reshape.17.refs_2_ = s32[1,768]{1,0:T(1,128)} reshape(s32[768]{0:T(1024)} %param.18) | data formatting | bytes 6144 | tf_op jit(solution)/shard_map/reshape | solution.py:462
  3.8 118.5 %shard_map.100 = bf16[12,8,2,8,128]{4,3,2,1,0:T(8,128)(2,1)} custom-call(s32[1,768]{1,0:T(1,128)} %reshape.15.refs_0_, s32[1,768]{1,0:T(1,128)} %reshape.16.refs_1_, s32[1,768]{1,0:T(1,128)} %reshape.17.refs_2_, f32[1,128]{1,0:T(1,128)} %constant.2.clone.refs_3_, bf16[12,16,1024]{2,1,0:T(8,128)(2,1)} %refs_4_.1, bf16[1024,1024]{1,0:T(8,128)(2,1)} %refs_5_.1, ...), custom_call_target="tpu_custom_call" | custom-call | tf_op jit(solution)/shard_map/pallas_call | solution.py:450
  122.3 1.2 copy.11
  123.5 0.8 reshape.19

commit v3 on v2

v3 whole, which is shorter than its diff:
```python
import jax
import jax.numpy as jnp
import numpy as np
from jax import lax
from jax.experimental import pallas as pl
from jax.experimental.pallas import tpu as pltpu
from jax.sharding import PartitionSpec as P

HEAD_DIM = 128
SLOTS = 16
CAP = 3
rotary_base = 500000.0
floor_score = -1e30
MESH = pl.DeviceIdType.MESH
SEND, RECV, BACK, SEAT, LENS, CNTS, TABLE = 0, 24, 120, 312, 328, 344, 360

GROUPS = (4, 4)
N_GROUPS = len(GROUPS)
HALF = SLOTS // 2
TOKENS = 12 * HALF
RUNS = ((0, 0, 1280), (1, 0, 768), (1, 768, 512))
N_RUNS = len(RUNS)
PLUS, MINUS = 0, 1
MESSAGES = ((1, 4), (0, 3), (1, 3), (0, 2), (1, 2), (0, 1), (1, 1))
OFFSETS = (4, 3, -3, 2, -2, 1, -1, 0)


def message_index(direction, half, distance):
    long = 1 if half == direction else 0
    return MESSAGES.index((long, distance))


def whole_wait(ref, sem):
    pltpu.make_async_copy(ref, ref, sem).wait()


def kernel(*refs):
    refs = list(refs)
    take = lambda n: [refs.pop(0) for _ in range(n)]
    agents, some_counts, some_lengths, frequency, rows, wq, wk, wv, keys, values = take(10)
    (out,) = take(1)
    table, idx, cosine, sine = take(4)
    outg, arrv0, arrv1, xg, wbuf, kbuf, vbuf, kn, vn = take(9)
    arrv = (arrv0, arrv1)
    sbuf = [take(2) for _ in range(N_RUNS)]
    rbuf = [take(2) for _ in range(N_RUNS)]
    qs, zs, zr, bo, inc = (take(N_GROUPS) for _ in range(5))
    local_sem, d_send, d_recv, ag_send, ag_recv, rs_send, rs_recv, z_send, z_recv, b_send, b_recv = take(11)

    g = lax.axis_index("grp")
    r = lax.axis_index("row")
    c = lax.axis_index("col")
    me = g * 8 + c

    loads = [
        pltpu.make_async_copy(wk, wbuf.at[:, pl.ds(0, HEAD_DIM)], local_sem.at[0]),
        pltpu.make_async_copy(wv, wbuf.at[:, pl.ds(HEAD_DIM, HEAD_DIM)], local_sem.at[1]),
        pltpu.make_async_copy(wq, wbuf.at[:, pl.ds(2 * HEAD_DIM, 1024)], local_sem.at[2]),
        pltpu.make_async_copy(keys, kbuf, local_sem.at[3]),
        pltpu.make_async_copy(values, vbuf, local_sem.at[4]),
    ]
    for load in loads:
        load.start()

    barrier = pltpu.get_barrier_semaphore()
    for i in range(8):
        for o in range(8):
            if (i, o) != (0, 0):
                pl.semaphore_signal(
                    barrier, inc=1, device_id=(lax.rem(g + i, 8), r, lax.rem(c + o, 8)), device_id_type=MESH
                )
    for i in range(1, 8):
        pl.semaphore_signal(barrier, inc=1, device_id=(g, lax.rem(r + i, 8), c), device_id_type=MESH)

    ra, all_counts, all_lengths = (n[...].reshape(1, 768) for n in (agents, some_counts, some_lengths))
    flat = lax.broadcasted_iota(jnp.int32, (1, 768), 1)
    region = lax.shift_right_logical(flat * 5462, 16)
    within = flat - region * 12
    served = lax.shift_right_logical(ra * 683, 16)
    bucket = jnp.zeros((1, 768), jnp.int32)
    for d in range(1, 12):
        same = (pltpu.roll(served, d, 1) == served) & (within >= d)
        bucket = bucket + same.astype(jnp.int32)
    place = region * CAP + bucket
    seat = served * CAP + bucket

    def pick(count, chosen, offset, values, most):
        want = lax.broadcasted_iota(jnp.int32, (count, 768), 0) + offset
        hit = jnp.broadcast_to(chosen, (count, 768)) == want
        total = jnp.sum(jnp.where(hit, jnp.broadcast_to(values, (count, 768)), 0), axis=1, keepdims=True)
        return jnp.broadcast_to(jnp.clip(total, 0, most), (count, 128))

    table[SEND : SEND + 24] = pick(24, jnp.where(region == me, seat, -1), 0, within, 11)
    table[RECV : RECV + 96] = pick(96, ra, g * 96, place, 64 * CAP - 1)
    table[BACK : BACK + 192] = pick(192, jnp.where(served == g, place, -1), 0, ra - g * 96, 95)
    table[SEAT : SEAT + 16] = pick(16, flat, me * 12, seat, 8 * CAP - 1)
    table[LENS : LENS + 16] = pick(16, flat, g * 96 + r * 12, all_lengths, 512)
    table[CNTS : CNTS + 16] = pick(16, flat, g * 96 + r * 12, all_counts, SLOTS)
    to_scalars = pltpu.make_async_copy(table, idx, local_sem.at[5])
    to_scalars.start()
    to_scalars.wait()

    def fill(s, target_group):
        for k in range(CAP):
            j = idx[SEND + target_group * CAP + k, 0]
            row = rows[j, s]
            for cc in range(8):
                outg[s, target_group * 8 + cc, k] = row[:, cc * 128 : (cc + 1) * 128]

    order = (4, 3, 5, 2, 6, 1, 7, 0)
    fill(0, lax.rem(g + order[0], 8))
    pl.semaphore_wait(barrier, 70)

    def dispatch(s):
        for n, i in enumerate(order):
            tg = lax.rem(g + i, 8)
            if n or s:
                fill(s, tg)
            for o in range(8):
                tc = lax.rem(c + o, 8)
                if (i, o) == (0, 0):
                    arrv[s][me] = outg[s, me]
                    continue
                pltpu.make_async_remote_copy(
                    src_ref=outg.at[s, tg * 8 + tc],
                    dst_ref=arrv[s].at[me],
                    send_sem=d_send.at[s],
                    recv_sem=d_recv.at[s],
                    device_id=(tg, r, tc),
                    device_id_type=MESH,
                ).start()

    def dispatch_wait(s):
        whole_wait(arrv[s].at[pl.ds(0, 63)], d_recv.at[s])

    dispatch(0)
    dispatch(1)

    slots = lax.broadcasted_iota(jnp.int32, (HALF, 128), 0)
    lanes = lax.broadcasted_iota(jnp.int32, (HALF, 128), 1)
    for s in range(2):
        for a in range(12):
            angle = (slots + (idx[LENS + a, 0] + s * HALF)).astype(jnp.float32) * frequency[...]
            cosine[s, a * HALF : (a + 1) * HALF] = jnp.cos(angle)
            turn = jnp.sin(angle)
            sine[s, a * HALF : (a + 1) * HALF] = jnp.where(lanes < 64, -turn, turn)

    x, p = lax.div(c, 2), lax.rem(c, 2)
    ahead = lax.rem(x + 1 + 2 * p, 4) * 2 + p
    behind = lax.rem(x + 3 + 2 * p, 4) * 2 + p
    far = lax.rem(x + 2, 4) * 2 + p
    sibling = c + 1 - 2 * p
    block_of = [lax.rem(r + o + 8, 8) for o in OFFSETS]

    def ag_copy(s, t, origin, target, kind):
        k = block_of[t]
        return pltpu.make_async_remote_copy(
            src_ref=xg.at[s, k, origin],
            dst_ref=xg.at[s, k, origin],
            send_sem=ag_send.at[s],
            recv_sem=ag_recv.at[s, t, kind],
            device_id=(g, r, target),
            device_id_type=MESH,
        )

    def ag_wait(s, t, kind):
        whole_wait(xg.at[s, block_of[t], c], ag_recv.at[s, t, kind])

    def ag_start(s, *ts):
        for t in ts:
            k = block_of[t]
            for a in range(12):
                seat = idx[RECV + k * 12 + a, 0]
                xg[s, k, c, a] = arrv[s][lax.div(seat, CAP), lax.rem(seat, CAP)]
            ag_copy(s, t, c, ahead, 1).start()
            ag_copy(s, t, c, behind, 2).start()
            ag_copy(s, t, c, sibling, 0).start()

    def ag_first(s, *ts):
        for t in ts:
            ag_wait(s, t, 1)
            ag_copy(s, t, behind, ahead, 3).start()
            ag_copy(s, t, behind, sibling, 4).start()
            ag_wait(s, t, 2)
            ag_copy(s, t, ahead, sibling, 5).start()

    def ag_second(s, *ts):
        for t in ts:
            ag_wait(s, t, 3)
            ag_copy(s, t, far, sibling, 6).start()

    def ag_finish(s, *ts):
        for t in ts:
            for kind in (0, 4, 5, 6):
                ag_wait(s, t, kind)

    def tokens(s, t):
        k = block_of[t]
        return jnp.concatenate([xg[s, k, cc].reshape(TOKENS, 128) for cc in range(8)], axis=1)

    up, down = lax.rem(r + 1, 8), lax.rem(r + 7, 8)
    toward = (up, down)

    def partial(run, half, t):
        s, first, width = RUNS[run]
        width = width // 2
        at = pl.ds(first + half * width, width)
        return jnp.dot(tokens(s, t), wbuf[:, at], preferred_element_type=jnp.float32)

    def rs_wait(run, direction, m):
        whole_wait(rbuf[run][direction].at[m], rs_recv.at[run, direction, m])

    def rs_step(run, m):
        is_long, distance = MESSAGES[m]
        for direction in (PLUS, MINUS):
            half = direction if is_long else 1 - direction
            t = OFFSETS.index(distance if direction == PLUS or distance == 4 else -distance)
            part = partial(run, half, t)
            if (is_long, distance + 1) in MESSAGES:
                before = MESSAGES.index((is_long, distance + 1))
                rs_wait(run, direction, before)
                part = part + rbuf[run][direction][before].astype(jnp.float32)
            sbuf[run][direction][m] = part.astype(jnp.bfloat16)
            pltpu.make_async_remote_copy(
                src_ref=sbuf[run][direction].at[m],
                dst_ref=rbuf[run][direction].at[m],
                send_sem=rs_send.at[run, direction],
                recv_sem=rs_recv.at[run, direction, m],
                device_id=(g, toward[direction], c),
                device_id_type=MESH,
            ).start()

    def rotate(u, s):
        return u * cosine[s] + pltpu.roll(u, 64, 1) * sine[s]

    def finish(run):
        s, first, width = RUNS[run]
        blocks = width // 256
        for half in (0, 1):
            own = partial(run, half, 7)
            for direction in (PLUS, MINUS):
                m = message_index(direction, half, 1)
                rs_wait(run, direction, m)
                own = own + rbuf[run][direction][m].astype(jnp.float32)
            for b in range(blocks):
                piece = own[:, b * 128 : (b + 1) * 128]
                head = first // 128 + half * blocks + b - 2
                if head == -2:
                    kn[:, s] = rotate(piece, s).astype(jnp.bfloat16).reshape(12, HALF, 128)
                elif head == -1:
                    vn[:, s] = piece.astype(jnp.bfloat16).reshape(12, HALF, 128)
                else:
                    gi, at = divmod(head, GROUPS[0])
                    qs[gi][:, at, s] = rotate(piece, s).astype(jnp.bfloat16).reshape(12, HALF, 128)

    def attend(gi):
        heads = GROUPS[gi]
        n = heads * SLOTS
        scale = HEAD_DIM ** (-0.5) * float(np.log2(np.e))
        row_s = lax.broadcasted_iota(jnp.int32, (n, SLOTS), 0) % SLOTS
        col_t = lax.broadcasted_iota(jnp.int32, (n, SLOTS), 1)
        causal = col_t <= row_s
        place = lax.broadcasted_iota(jnp.int32, (n, 512), 1)
        slot = lax.broadcasted_iota(jnp.int32, (n, 128), 0) % SLOTS
        i = lax.broadcasted_iota(jnp.int32, (n, n), 0)
        j = lax.broadcasted_iota(jnp.int32, (n, n), 1)
        pair, rest = i // (2 * heads), i % (2 * heads)
        swap = ((rest // 2) * SLOTS + pair * 2 + rest % 2 == j).astype(jnp.float32).astype(jnp.bfloat16)
        last = (((1,), (1,)), ((), ()))

        def one(a, _):
            length, count = idx[LENS + a, 0], idx[CNTS + a, 0]
            q = qs[gi][a].reshape(n, 128)
            s1 = lax.dot_general(q, kbuf[a], last, preferred_element_type=jnp.float32) * scale
            s2 = lax.dot_general(q, kn[a].reshape(SLOTS, 128), last, preferred_element_type=jnp.float32) * scale
            s1 = jnp.where(place < length, s1, floor_score)
            s2 = jnp.where(causal & (col_t < count), s2, floor_score)
            top = jnp.maximum(jnp.max(s1, axis=1, keepdims=True), jnp.max(s2, axis=1, keepdims=True))
            p1, p2 = jnp.exp2(s1 - top), jnp.exp2(s2 - top)
            den = jnp.sum(p1, axis=1, keepdims=True) + jnp.sum(p2, axis=1, keepdims=True)
            mixed = jnp.dot(p1.astype(jnp.bfloat16), vbuf[a], preferred_element_type=jnp.float32)
            mixed = mixed + jnp.dot(p2.astype(jnp.bfloat16), vn[a].reshape(SLOTS, 128), preferred_element_type=jnp.float32)
            mixed = jnp.where(slot < count, mixed / den, 0.0).astype(jnp.bfloat16)
            swapped = jnp.dot(swap, mixed, preferred_element_type=jnp.float32).astype(jnp.bfloat16)
            zs[gi][:, a] = swapped.reshape(8, 2 * heads, 128)
            return 0

        lax.fori_loop(0, 12, one, 0, unroll=2)

    def z_start(gi):
        for i in (4, 3, 5, 2, 6, 1, 7):
            other = lax.rem(r + i, 8)
            pltpu.make_async_remote_copy(
                src_ref=zs[gi].at[other],
                dst_ref=zr[gi].at[r],
                send_sem=z_send.at[gi],
                recv_sem=z_recv.at[gi],
                device_id=(g, other, c),
                device_id_type=MESH,
            ).start()
        zr[gi][r] = zs[gi][r]

    def back_start(gi):
        whole_wait(zr[gi].at[pl.ds(0, 7)], z_recv.at[gi])
        for i in order:
            tg = lax.rem(g + i, 8)
            for o in range(8):
                tc = lax.rem(c + o, 8)
                target = tg * 8 + tc
                for k in range(CAP):
                    a = idx[BACK + target * CAP + k, 0]
                    bo[gi][target, k] = zr[gi][lax.div(a, 12), lax.rem(a, 12)]
                if (i, o) == (0, 0):
                    inc[gi][g, c] = bo[gi][target]
                    continue
                pltpu.make_async_remote_copy(
                    src_ref=bo[gi].at[target],
                    dst_ref=inc[gi].at[g, c],
                    send_sem=b_send.at[gi],
                    recv_sem=b_recv.at[gi],
                    device_id=(tg, r, tc),
                    device_id_type=MESH,
                ).start()

    def back_finish(gi):
        whole_wait(bo[gi].at[pl.ds(0, 63)], b_recv.at[gi])
        for j in range(12):
            seat_j = idx[SEAT + j, 0]
            out[j, :, gi] = inc[gi][lax.div(seat_j, CAP), :, lax.rem(seat_j, CAP)]

    dispatch_wait(0)
    ag_start(0, 0, 1, 2)
    ag_first(0, 0)
    ag_start(0, 3, 4)
    ag_second(0, 0)
    for load in loads[:3]:
        load.wait()
    ag_first(0, 1, 2)
    ag_finish(0, 0)
    rs_step(0, 0)
    ag_start(0, 5, 6, 7)
    ag_second(0, 1, 2)
    ag_first(0, 3, 4)
    ag_finish(0, 1, 2)
    rs_step(0, 1)
    ag_second(0, 3, 4)
    rs_step(0, 2)
    ag_first(0, 5, 6, 7)
    ag_finish(0, 3, 4)
    rs_step(0, 3)
    ag_second(0, 5, 6, 7)
    ag_finish(0, 5, 6, 7)
    dispatch_wait(1)
    ag_start(1, 0, 1, 2, 3, 4)
    rs_step(0, 4)
    ag_first(1, 0, 1, 2)
    ag_start(1, 5, 6, 7)
    rs_step(0, 5)
    ag_second(1, 0, 1, 2)
    ag_first(1, 3, 4)
    rs_step(0, 6)
    ag_finish(1, 0, 1, 2)
    rs_step(1, 0)
    rs_step(1, 1)
    ag_second(1, 3, 4)
    ag_first(1, 5, 6, 7)
    for load in loads[3:]:
        load.wait()
    finish(0)
    rs_step(1, 2)
    ag_second(1, 5, 6, 7)
    ag_finish(1, 3, 4)
    rs_step(1, 3)
    ag_finish(1, 5, 6, 7)
    rs_step(1, 4)
    rs_step(1, 5)
    rs_step(1, 6)
    rs_step(2, 0)
    rs_step(2, 1)
    finish(1)
    rs_step(2, 2)
    attend(0)
    z_start(0)
    rs_step(2, 3)
    rs_step(2, 4)
    back_start(0)
    rs_step(2, 5)
    rs_step(2, 6)
    finish(2)
    attend(1)
    z_start(1)
    back_finish(0)
    back_start(1)
    back_finish(1)

    for s in range(2):
        whole_wait(outg.at[s, pl.ds(0, 63)], d_send.at[s])
        whole_wait(xg.at[s, pl.ds(0, 7)], ag_send.at[s])
    for run in range(N_RUNS):
        for direction in (PLUS, MINUS):
            whole_wait(sbuf[run][direction], rs_send.at[run, direction])
    for gi in range(N_GROUPS):
        whole_wait(zs[gi].at[pl.ds(0, 7)], z_send.at[gi])
        whole_wait(bo[gi].at[pl.ds(0, 63)], b_send.at[gi])


def local(
    new_rows,
    query_weight,
    key_weight,
    value_weight,
    cache_keys,
    cache_values,
    region_agents,
    new_counts,
    cache_lengths,
):
    half_frequency = rotary_base ** (-np.arange(64) * (2.0 / HEAD_DIM))
    frequency = jnp.asarray(np.tile(half_frequency, 2).astype(np.float32).reshape(1, 128))
    bf, vmem = jnp.bfloat16, pltpu.VMEM
    scratch = [
        vmem((TABLE, 128), jnp.int32),
        pltpu.SMEM((TABLE, 128), jnp.int32),
        vmem((2, TOKENS, 128), jnp.float32),
        vmem((2, TOKENS, 128), jnp.float32),
        vmem((2, 64, CAP, HALF, 128), bf),
        vmem((64, CAP, HALF, 128), bf),
        vmem((64, CAP, HALF, 128), bf),
        vmem((2, 8, 8, 12, HALF, 128), bf),
        vmem((1024, 1280), bf),
        vmem((12, 512, 128), bf),
        vmem((12, 512, 128), bf),
        vmem((12, 2, HALF, 128), bf),
        vmem((12, 2, HALF, 128), bf),
    ]
    for _ in range(2):
        for run in RUNS:
            scratch += [vmem((7, TOKENS, run[2] // 2), bf)] * 2
    scratch += [vmem((12, h, 2, HALF, 128), bf) for h in GROUPS]
    scratch += [vmem((8, 12, 2 * h, 128), bf) for h in GROUPS] * 2
    scratch += [vmem((64, CAP, 2 * h, 128), bf) for h in GROUPS]
    scratch += [vmem((8, 8, CAP, 2 * h, 128), bf) for h in GROUPS]
    dma = pltpu.SemaphoreType.DMA
    scratch += [
        dma((6,)),
        dma((2,)),
        dma((2,)),
        dma((2,)),
        dma((2, 8, 7)),
        dma((N_RUNS, 2)),
        dma((N_RUNS, 2, 7)),
        dma((N_GROUPS,)),
        dma((N_GROUPS,)),
        dma((N_GROUPS,)),
        dma((N_GROUPS,)),
    ]
    in_vmem = pl.BlockSpec(memory_space=pltpu.VMEM)
    anywhere = pl.BlockSpec(memory_space=pl.ANY)
    heads = GROUPS[0]
    result = pl.pallas_call(
        kernel,
        out_shape=jax.ShapeDtypeStruct((12, 8, N_GROUPS, 2 * heads, 128), bf),
        in_specs=[in_vmem] * 5 + [anywhere] * 5,
        out_specs=in_vmem,
        scratch_shapes=scratch,
        compiler_params=pltpu.CompilerParams(
            collective_id=0, has_side_effects=True, vmem_limit_bytes=56 * 2**20
        ),
    )(
        region_agents,
        new_counts,
        cache_lengths,
        frequency,
        new_rows.reshape(12, 2, HALF, 1024),
        query_weight,
        key_weight,
        value_weight,
        cache_keys,
        cache_values,
    )
    return result.reshape(12, 64, 2, HEAD_DIM).transpose(0, 2, 1, 3).reshape(12, 2, 8192)


def solution(mesh):
    placed = (
        P(("grp", "col"), None, "row"),
        P("row", "col"),
        P("row", "col"),
        P("row", "col"),
        P(("grp", "row"), None, "col"),
        P(("grp", "row"), None, "col"),
        P(),
        P(),
        P(),
    )
    return jax.shard_map(
        local, mesh=mesh, in_specs=placed, out_specs=P(("grp", "col"), "row", None), check_vma=False
    )
```

time: 125 us -> 121 us (0.968)
  local copies, waits for them, and re-layouts: 5.84 us -> 2.07 us
    reshape x4 -> x0, local copies, waits for them, and re-layouts: 4.65 us -> none  [the longest x1 1.28 us: local(): cache_lengths.reshape(1, 768)]
    unnamed x0 -> x1, local copies, waits for them, and re-layouts: none -> 2.07 us
where the time goes in v3:
time: 121 us
  Pallas kernels  119 us (98%)
  local copies, waits for them, and re-layouts  2.07 us (2%)
    pallas_call x1, Pallas kernels, local(): pl.pallas_call(kernel, out_shape=jax.ShapeDtypeStruct((12, 8, N_GROUPS, 2...  119 us

profile of v3, /device:TPU:1, one launch (start us, length us, event | category | flops | bytes accessed | tf_op | source)
XLA Modules:
  0.0 120.9 jit_solution(6496635506351397725)
XLA Ops:
  0.0 118.8 %shard_map.100 = bf16[12,8,2,8,128]{4,3,2,1,0:T(8,128)(2,1)} custom-call(s32[768]{0:T(1024)} %refs_0_.1, s32[768]{0:T(1024)} %refs_1_.1, s32[768]{0:T(1024)} %refs_2_.1, f32[1,128]{1,0:T(1,128)} %constant.2.clone.refs_3_, bf16[12,2,8,1024]{3,2,1,0:T(8,128)(2,1)} %bitcast.7, bf16[1024,1024]{1,0:T(8,128)(2,1)} %refs_5_.1, bf16[1024,128]{1,0:T(8,128)(2,1)} %refs_6_.1, ...), custom_call_target="tpu_custom_call" | custom-call | tf_op jit(solution)/shard_map/pallas_call | solution.py:460
  118.8 2.1 %copy.13 = bf16[12,2,8192]{2,1,0:T(2,128)(2,1)} copy(bf16[12,2,8192]{2,1,0:T(2,128)(2,1)} %bitcast.6) | data formatting | bytes 786432

commit v4 on v3

--- a/solution.py
+++ b/solution.py
@@ -12,7 +12,7 @@
 rotary_base = 500000.0
 floor_score = -1e30
 MESH = pl.DeviceIdType.MESH
-SEND, RECV, BACK, SEAT, LENS, CNTS, TABLE = 0, 24, 120, 312, 328, 344, 360
+SEND, RECV, BACK, SEAT, LENS, CNTS, TABLE = 0, 24, 120, 312, 328, 344, 384
 
 GROUPS = (4, 4)
 N_GROUPS = len(GROUPS)
@@ -39,13 +39,13 @@
     take = lambda n: [refs.pop(0) for _ in range(n)]
     agents, some_counts, some_lengths, frequency, rows, wq, wk, wv, keys, values = take(10)
     (out,) = take(1)
-    table, idx, cosine, sine = take(4)
+    table, compact, idx, cosine, sine = take(5)
     outg, arrv0, arrv1, xg, wbuf, kbuf, vbuf, kn, vn = take(9)
     arrv = (arrv0, arrv1)
     sbuf = [take(2) for _ in range(N_RUNS)]
     rbuf = [take(2) for _ in range(N_RUNS)]
     qs, zs, zr, bo, inc = (take(N_GROUPS) for _ in range(5))
-    local_sem, d_send, d_recv, ag_send, ag_recv, rs_send, rs_recv, z_send, z_recv, b_send, b_recv = take(11)
+    local_sem, d_send, d_recv, ag_send, ag_recv, rs_send_sem, rs_recv, z_send, z_recv, b_send, b_recv = take(11)
 
     g = lax.axis_index("grp")
     r = lax.axis_index("row")
@@ -96,13 +96,20 @@
     table[SEAT : SEAT + 16] = pick(16, flat, me * 12, seat, 8 * CAP - 1)
     table[LENS : LENS + 16] = pick(16, flat, g * 96 + r * 12, all_lengths, 512)
     table[CNTS : CNTS + 16] = pick(16, flat, g * 96 + r * 12, all_counts, SLOTS)
-    to_scalars = pltpu.make_async_copy(table, idx, local_sem.at[5])
+    table[CNTS + 16 : TABLE] = jnp.zeros((TABLE - CNTS - 16, 128), jnp.int32)
+    square = table[...].reshape(3, 128, 128)
+    diagonal = lax.broadcasted_iota(jnp.int32, (3, 128, 128), 1) == lax.broadcasted_iota(jnp.int32, (3, 128, 128), 2)
+    compact[...] = jnp.sum(jnp.where(diagonal, square, 0), axis=1)
+    to_scalars = pltpu.make_async_copy(compact, idx, local_sem.at[5])
     to_scalars.start()
     to_scalars.wait()
 
+    def number(at):
+        return idx[at // 128, at % 128] if isinstance(at, int) else idx[lax.div(at, 128), lax.rem(at, 128)]
+
     def fill(s, target_group):
         for k in range(CAP):
-            j = idx[SEND + target_group * CAP + k, 0]
+            j = number(SEND + target_group * CAP + k)
             row = rows[j, s]
             for cc in range(8):
                 outg[s, target_group * 8 + cc, k] = row[:, cc * 128 : (cc + 1) * 128]
@@ -114,7 +121,7 @@
     def dispatch(s):
         for n, i in enumerate(order):
             tg = lax.rem(g + i, 8)
-            if n or s:
+            if n and s == 0:
                 fill(s, tg)
             for o in range(8):
                 tc = lax.rem(c + o, 8)
@@ -134,13 +141,14 @@
         whole_wait(arrv[s].at[pl.ds(0, 63)], d_recv.at[s])
 
     dispatch(0)
-    dispatch(1)
+    for i in order:
+        fill(1, lax.rem(g + i, 8))
 
     slots = lax.broadcasted_iota(jnp.int32, (HALF, 128), 0)
     lanes = lax.broadcasted_iota(jnp.int32, (HALF, 128), 1)
     for s in range(2):
         for a in range(12):
-            angle = (slots + (idx[LENS + a, 0] + s * HALF)).astype(jnp.float32) * frequency[...]
+            angle = (slots + (number(LENS + a) + s * HALF)).astype(jnp.float32) * frequency[...]
             cosine[s, a * HALF : (a + 1) * HALF] = jnp.cos(angle)
             turn = jnp.sin(angle)
             sine[s, a * HALF : (a + 1) * HALF] = jnp.where(lanes < 64, -turn, turn)
@@ -166,15 +174,26 @@
     def ag_wait(s, t, kind):
         whole_wait(xg.at[s, block_of[t], c], ag_recv.at[s, t, kind])
 
+    def land(s, k):
+        for a in range(12):
+            seat = number(RECV + k * 12 + a)
+            xg[s, k, c, a] = arrv[s][lax.div(seat, CAP), lax.rem(seat, CAP)]
+
     def ag_start(s, *ts):
         for t in ts:
-            k = block_of[t]
-            for a in range(12):
-                seat = idx[RECV + k * 12 + a, 0]
-                xg[s, k, c, a] = arrv[s][lax.div(seat, CAP), lax.rem(seat, CAP)]
+            land(s, block_of[t])
             ag_copy(s, t, c, ahead, 1).start()
             ag_copy(s, t, c, behind, 2).start()
             ag_copy(s, t, c, sibling, 0).start()
+
+    def ag_direct(s, t):
+        k = block_of[t]
+        land(s, k)
+        for i in (3, 4, 5, 2, 6, 7, 1):
+            ag_copy(s, t, c, lax.rem(c + i, 8), 0).start()
+
+    def ag_direct_wait(s, t):
+        whole_wait(xg.at[s, block_of[t], pl.ds(0, 7)], ag_recv.at[s, t, 0])
 
     def ag_first(s, *ts):
         for t in ts:
@@ -210,21 +229,26 @@
     def rs_wait(run, direction, m):
         whole_wait(rbuf[run][direction].at[m], rs_recv.at[run, direction, m])
 
-    def rs_step(run, m):
+    def rs_dot(run, *ms):
+        for m in ms:
+            is_long, distance = MESSAGES[m]
+            for direction in (PLUS, MINUS):
+                half = direction if is_long else 1 - direction
+                t = OFFSETS.index(distance if direction == PLUS or distance == 4 else -distance)
+                sbuf[run][direction][m] = partial(run, half, t).astype(jnp.bfloat16)
+
+    def rs_send(run, m):
         is_long, distance = MESSAGES[m]
         for direction in (PLUS, MINUS):
-            half = direction if is_long else 1 - direction
-            t = OFFSETS.index(distance if direction == PLUS or distance == 4 else -distance)
-            part = partial(run, half, t)
             if (is_long, distance + 1) in MESSAGES:
                 before = MESSAGES.index((is_long, distance + 1))
                 rs_wait(run, direction, before)
-                part = part + rbuf[run][direction][before].astype(jnp.float32)
-            sbuf[run][direction][m] = part.astype(jnp.bfloat16)
+                total = sbuf[run][direction][m].astype(jnp.float32) + rbuf[run][direction][before].astype(jnp.float32)
+                sbuf[run][direction][m] = total.astype(jnp.bfloat16)
             pltpu.make_async_remote_copy(
                 src_ref=sbuf[run][direction].at[m],
                 dst_ref=rbuf[run][direction].at[m],
-                send_sem=rs_send.at[run, direction],
+                send_sem=rs_send_sem.at[run, direction],
                 recv_sem=rs_recv.at[run, direction, m],
                 device_id=(g, toward[direction], c),
                 device_id_type=MESH,
@@ -253,6 +277,20 @@
                     gi, at = divmod(head, GROUPS[0])
                     qs[gi][:, at, s] = rotate(piece, s).astype(jnp.bfloat16).reshape(12, HALF, 128)
 
+    def z_start(gi, part):
+        some = pl.ds(part * 6, 6)
+        for i in (4, 3, 5, 2, 6, 1, 7):
+            other = lax.rem(r + i, 8)
+            pltpu.make_async_remote_copy(
+                src_ref=zs[gi].at[other, some],
+                dst_ref=zr[gi].at[r, some],
+                send_sem=z_send.at[gi],
+                recv_sem=z_recv.at[gi],
+                device_id=(g, other, c),
+                device_id_type=MESH,
+            ).start()
+        zr[gi][r, some] = zs[gi][r, some]
+
     def attend(gi):
         heads = GROUPS[gi]
         n = heads * SLOTS
@@ -269,7 +307,7 @@
         last = (((1,), (1,)), ((), ()))
 
         def one(a, _):
-            length, count = idx[LENS + a, 0], idx[CNTS + a, 0]
+            length, count = number(LENS + a), number(CNTS + a)
             q = qs[gi][a].reshape(n, 128)
             s1 = lax.dot_general(q, kbuf[a], last, preferred_element_type=jnp.float32) * scale
             s2 = lax.dot_general(q, kn[a].reshape(SLOTS, 128), last, preferred_element_type=jnp.float32) * scale
@@ -285,20 +323,9 @@
             zs[gi][:, a] = swapped.reshape(8, 2 * heads, 128)
             return 0
 
-        lax.fori_loop(0, 12, one, 0, unroll=2)
-
-    def z_start(gi):
-        for i in (4, 3, 5, 2, 6, 1, 7):
-            other = lax.rem(r + i, 8)
-            pltpu.make_async_remote_copy(
-                src_ref=zs[gi].at[other],
-                dst_ref=zr[gi].at[r],
-                send_sem=z_send.at[gi],
-                recv_sem=z_recv.at[gi],
-                device_id=(g, other, c),
-                device_id_type=MESH,
-            ).start()
-        zr[gi][r] = zs[gi][r]
+        for part in range(2):
+            lax.fori_loop(part * 6, part * 6 + 6, one, 0, unroll=2)
+            z_start(gi, part)
 
     def back_start(gi):
         whole_wait(zr[gi].at[pl.ds(0, 7)], z_recv.at[gi])
@@ -308,7 +335,7 @@
                 tc = lax.rem(c + o, 8)
                 target = tg * 8 + tc
                 for k in range(CAP):
-                    a = idx[BACK + target * CAP + k, 0]
+                    a = number(BACK + target * CAP + k)
                     bo[gi][target, k] = zr[gi][lax.div(a, 12), lax.rem(a, 12)]
                 if (i, o) == (0, 0):
                     inc[gi][g, c] = bo[gi][target]
@@ -325,70 +352,88 @@
     def back_finish(gi):
         whole_wait(bo[gi].at[pl.ds(0, 63)], b_recv.at[gi])
         for j in range(12):
-            seat_j = idx[SEAT + j, 0]
+            seat_j = number(SEAT + j)
             out[j, :, gi] = inc[gi][lax.div(seat_j, CAP), :, lax.rem(seat_j, CAP)]
 
     dispatch_wait(0)
-    ag_start(0, 0, 1, 2)
-    ag_first(0, 0)
+    ag_direct(0, 0)
+    ag_start(0, 1, 2)
+    dispatch(1)
     ag_start(0, 3, 4)
-    ag_second(0, 0)
     for load in loads[:3]:
         load.wait()
+    ag_direct_wait(0, 0)
+    rs_dot(0, 0)
+    rs_send(0, 0)
     ag_first(0, 1, 2)
-    ag_finish(0, 0)
-    rs_step(0, 0)
     ag_start(0, 5, 6, 7)
     ag_second(0, 1, 2)
+    ag_finish(0, 1, 2)
+    rs_dot(0, 1)
+    rs_send(0, 1)
     ag_first(0, 3, 4)
-    ag_finish(0, 1, 2)
-    rs_step(0, 1)
+    rs_dot(0, 2)
     ag_second(0, 3, 4)
-    rs_step(0, 2)
+    ag_finish(0, 3, 4)
+    rs_send(0, 2)
+    rs_dot(0, 3)
     ag_first(0, 5, 6, 7)
-    ag_finish(0, 3, 4)
-    rs_step(0, 3)
+    rs_send(0, 3)
+    rs_dot(0, 4)
     ag_second(0, 5, 6, 7)
+    dispatch_wait(1)
+    ag_start(1, 0, 1, 2)
+    rs_send(0, 4)
     ag_finish(0, 5, 6, 7)
-    dispatch_wait(1)
-    ag_start(1, 0, 1, 2, 3, 4)
-    rs_step(0, 4)
+    rs_dot(0, 5, 6)
+    ag_start(1, 3, 4)
     ag_first(1, 0, 1, 2)
+    rs_send(0, 5)
     ag_start(1, 5, 6, 7)
-    rs_step(0, 5)
     ag_second(1, 0, 1, 2)
+    ag_finish(1, 0)
+    rs_dot(1, 0)
+    rs_send(1, 0)
+    rs_send(0, 6)
+    ag_finish(1, 1, 2)
+    rs_dot(1, 1)
+    rs_send(1, 1)
     ag_first(1, 3, 4)
-    rs_step(0, 6)
-    ag_finish(1, 0, 1, 2)
-    rs_step(1, 0)
-    rs_step(1, 1)
+    rs_dot(2, 0)
+    rs_dot(1, 2)
+    rs_send(2, 0)
     ag_second(1, 3, 4)
+    rs_send(1, 2)
     ag_first(1, 5, 6, 7)
+    ag_finish(1, 3, 4)
+    rs_dot(1, 3)
+    rs_dot(2, 1)
+    rs_send(1, 3)
+    rs_send(2, 1)
+    rs_dot(1, 4)
+    ag_second(1, 5, 6, 7)
     for load in loads[3:]:
         load.wait()
     finish(0)
-    rs_step(1, 2)
-    ag_second(1, 5, 6, 7)
-    ag_finish(1, 3, 4)
-    rs_step(1, 3)
+    rs_send(1, 4)
     ag_finish(1, 5, 6, 7)
-    rs_step(1, 4)
-    rs_step(1, 5)
-    rs_step(1, 6)
-    rs_step(2, 0)
-    rs_step(2, 1)
+    rs_dot(1, 5)
+    rs_dot(2, 2)
+    rs_send(1, 5)
+    rs_send(2, 2)
+    rs_dot(1, 6)
+    rs_dot(2, 3)
+    rs_send(1, 6)
+    rs_send(2, 3)
+    rs_dot(2, 4, 5, 6)
+    rs_send(2, 4)
     finish(1)
-    rs_step(2, 2)
+    rs_send(2, 5)
     attend(0)
-    z_start(0)
-    rs_step(2, 3)
-    rs_step(2, 4)
+    rs_send(2, 6)
     back_start(0)
-    rs_step(2, 5)
-    rs_step(2, 6)
     finish(2)
     attend(1)
-    z_start(1)
     back_finish(0)
     back_start(1)
     back_finish(1)
@@ -398,7 +443,7 @@
         whole_wait(xg.at[s, pl.ds(0, 7)], ag_send.at[s])
     for run in range(N_RUNS):
         for direction in (PLUS, MINUS):
-            whole_wait(sbuf[run][direction], rs_send.at[run, direction])
+            whole_wait(sbuf[run][direction], rs_send_sem.at[run, direction])
     for gi in range(N_GROUPS):
         whole_wait(zs[gi].at[pl.ds(0, 7)], z_send.at[gi])
         whole_wait(bo[gi].at[pl.ds(0, 63)], b_send.at[gi])
@@ -420,7 +465,8 @@
     bf, vmem = jnp.bfloat16, pltpu.VMEM
     scratch = [
         vmem((TABLE, 128), jnp.int32),
-        pltpu.SMEM((TABLE, 128), jnp.int32),
+        vmem((3, 128), jnp.int32),
+        pltpu.SMEM((3, 128), jnp.int32),
         vmem((2, TOKENS, 128), jnp.float32),
         vmem((2, TOKENS, 128), jnp.float32),
         vmem((2, 64, CAP, HALF, 128), bf),

time: 121 us -> 118 us (0.975)
  Pallas kernels: 119 us -> 116 us
    pallas_call x1, Pallas kernels: 119 us -> 116 us  [local(): pl.pallas_call(kernel, out_shape=jax.ShapeDtypeStruct((12, 8, N_GROUPS, 2...]
where the time goes in v4:
time: 118 us
  Pallas kernels  116 us (98%)
  local copies, waits for them, and re-layouts  2.07 us (2%)
    pallas_call x1, Pallas kernels, local(): pl.pallas_call(kernel, out_shape=jax.ShapeDtypeStruct((12, 8, N_GROUPS, 2...  116 us

profile of v4, /device:TPU:1, one launch (start us, length us, event | category | flops | bytes accessed | tf_op | source)
XLA Modules:
  0.0 118.0 jit_solution(12086343281710635442)
XLA Ops:
  0.0 116.0 %shard_map.100 = bf16[12,8,2,8,128]{4,3,2,1,0:T(8,128)(2,1)} custom-call(s32[768]{0:T(1024)} %refs_0_.1, s32[768]{0:T(1024)} %refs_1_.1, s32[768]{0:T(1024)} %refs_2_.1, f32[1,128]{1,0:T(1,128)} %constant.2.clone.refs_3_, bf16[12,2,8,1024]{3,2,1,0:T(8,128)(2,1)} %bitcast.7, bf16[1024,1024]{1,0:T(8,128)(2,1)} %refs_5_.1, bf16[1024,128]{1,0:T(8,128)(2,1)} %refs_6_.1, ...), custom_call_target="tpu_custom_call" | custom-call | tf_op jit(solution)/shard_map/pallas_call | solution.py:506
  116.0 2.1 %copy.13 = bf16[12,2,8192]{2,1,0:T(2,128)(2,1)} copy(bf16[12,2,8192]{2,1,0:T(2,128)(2,1)} %bitcast.6) | data formatting | bytes 786432

commit v5 on v4

--- a/solution.py
+++ b/solution.py
@@ -14,11 +14,11 @@
 MESH = pl.DeviceIdType.MESH
 SEND, RECV, BACK, SEAT, LENS, CNTS, TABLE = 0, 24, 120, 312, 328, 344, 384
 
-GROUPS = (4, 4)
-N_GROUPS = len(GROUPS)
+N_GROUPS = 2
+HEADS = 8
 HALF = SLOTS // 2
 TOKENS = 12 * HALF
-RUNS = ((0, 0, 1280), (1, 0, 768), (1, 768, 512))
+RUNS = ((0, 0, 1280), (1, 0, 256), (1, 256, 1024))
 N_RUNS = len(RUNS)
 PLUS, MINUS = 0, 1
 MESSAGES = ((1, 4), (0, 3), (1, 3), (0, 2), (1, 2), (0, 1), (1, 1))
@@ -40,7 +40,7 @@
     agents, some_counts, some_lengths, frequency, rows, wq, wk, wv, keys, values = take(10)
     (out,) = take(1)
     table, compact, idx, cosine, sine = take(5)
-    outg, arrv0, arrv1, xg, wbuf, kbuf, vbuf, kn, vn = take(9)
+    prow, outg, arrv0, arrv1, xg, wbuf, kbuf, vbuf, kn, vn = take(10)
     arrv = (arrv0, arrv1)
     sbuf = [take(2) for _ in range(N_RUNS)]
     rbuf = [take(2) for _ in range(N_RUNS)]
@@ -104,13 +104,20 @@
     to_scalars.start()
     to_scalars.wait()
 
+    to = lax.broadcasted_iota(jnp.int32, (SLOTS, SLOTS), 0)
+    of = lax.broadcasted_iota(jnp.int32, (SLOTS, SLOTS), 1)
+    apart = (2 * (to % HALF) + to // HALF == of).astype(jnp.float32).astype(jnp.bfloat16)
+    for j in range(12):
+        moved = jnp.dot(apart, rows[j], preferred_element_type=jnp.float32).astype(jnp.bfloat16)
+        prow[j] = moved.reshape(2, HALF, 1024)
+
     def number(at):
         return idx[at // 128, at % 128] if isinstance(at, int) else idx[lax.div(at, 128), lax.rem(at, 128)]
 
     def fill(s, target_group):
         for k in range(CAP):
             j = number(SEND + target_group * CAP + k)
-            row = rows[j, s]
+            row = prow[j, s]
             for cc in range(8):
                 outg[s, target_group * 8 + cc, k] = row[:, cc * 128 : (cc + 1) * 128]
 
@@ -148,7 +155,7 @@
     lanes = lax.broadcasted_iota(jnp.int32, (HALF, 128), 1)
     for s in range(2):
         for a in range(12):
-            angle = (slots + (number(LENS + a) + s * HALF)).astype(jnp.float32) * frequency[...]
+            angle = (2 * slots + (number(LENS + a) + s)).astype(jnp.float32) * frequency[...]
             cosine[s, a * HALF : (a + 1) * HALF] = jnp.cos(angle)
             turn = jnp.sin(angle)
             sine[s, a * HALF : (a + 1) * HALF] = jnp.where(lanes < 64, -turn, turn)
@@ -274,8 +281,7 @@
                 elif head == -1:
                     vn[:, s] = piece.astype(jnp.bfloat16).reshape(12, HALF, 128)
                 else:
-                    gi, at = divmod(head, GROUPS[0])
-                    qs[gi][:, at, s] = rotate(piece, s).astype(jnp.bfloat16).reshape(12, HALF, 128)
+                    qs[s][:, head] = rotate(piece, s).astype(jnp.bfloat16).reshape(12, HALF, 128)
 
     def z_start(gi, part):
         some = pl.ds(part * 6, 6)
@@ -291,19 +297,18 @@
             ).start()
         zr[gi][r, some] = zs[gi][r, some]
 
-    def attend(gi):
-        heads = GROUPS[gi]
-        n = heads * SLOTS
+    def attend(gi, *parts):
+        n = HEADS * HALF
         scale = HEAD_DIM ** (-0.5) * float(np.log2(np.e))
-        row_s = lax.broadcasted_iota(jnp.int32, (n, SLOTS), 0) % SLOTS
+        row_s = 2 * (lax.broadcasted_iota(jnp.int32, (n, SLOTS), 0) % HALF) + gi
         col_t = lax.broadcasted_iota(jnp.int32, (n, SLOTS), 1)
+        col_t = 2 * (col_t % HALF) + col_t // HALF
         causal = col_t <= row_s
         place = lax.broadcasted_iota(jnp.int32, (n, 512), 1)
-        slot = lax.broadcasted_iota(jnp.int32, (n, 128), 0) % SLOTS
+        slot = 2 * (lax.broadcasted_iota(jnp.int32, (n, 128), 0) % HALF) + gi
         i = lax.broadcasted_iota(jnp.int32, (n, n), 0)
         j = lax.broadcasted_iota(jnp.int32, (n, n), 1)
-        pair, rest = i // (2 * heads), i % (2 * heads)
-        swap = ((rest // 2) * SLOTS + pair * 2 + rest % 2 == j).astype(jnp.float32).astype(jnp.bfloat16)
+        swap = ((i % HEADS) * HALF + i // HEADS == j).astype(jnp.float32).astype(jnp.bfloat16)
         last = (((1,), (1,)), ((), ()))
 
         def one(a, _):
@@ -320,10 +325,10 @@
             mixed = mixed + jnp.dot(p2.astype(jnp.bfloat16), vn[a].reshape(SLOTS, 128), preferred_element_type=jnp.float32)
             mixed = jnp.where(slot < count, mixed / den, 0.0).astype(jnp.bfloat16)
             swapped = jnp.dot(swap, mixed, preferred_element_type=jnp.float32).astype(jnp.bfloat16)
-            zs[gi][:, a] = swapped.reshape(8, 2 * heads, 128)
+            zs[gi][:, a] = swapped.reshape(8, HEADS, 128)
             return 0
 
-        for part in range(2):
+        for part in parts:
             lax.fori_loop(part * 6, part * 6 + 6, one, 0, unroll=2)
             z_start(gi, part)
 
@@ -395,45 +400,45 @@
     rs_dot(1, 0)
     rs_send(1, 0)
     rs_send(0, 6)
+    rs_dot(2, 0)
     ag_finish(1, 1, 2)
     rs_dot(1, 1)
     rs_send(1, 1)
+    rs_send(2, 0)
+    rs_dot(1, 2)
     ag_first(1, 3, 4)
-    rs_dot(2, 0)
-    rs_dot(1, 2)
-    rs_send(2, 0)
+    rs_send(1, 2)
+    rs_dot(2, 1)
+    rs_send(2, 1)
     ag_second(1, 3, 4)
-    rs_send(1, 2)
     ag_first(1, 5, 6, 7)
     ag_finish(1, 3, 4)
-    rs_dot(1, 3)
-    rs_dot(2, 1)
+    rs_dot(1, 3, 4)
     rs_send(1, 3)
-    rs_send(2, 1)
-    rs_dot(1, 4)
+    rs_dot(2, 2)
     ag_second(1, 5, 6, 7)
     for load in loads[3:]:
         load.wait()
-    finish(0)
     rs_send(1, 4)
+    rs_send(2, 2)
     ag_finish(1, 5, 6, 7)
-    rs_dot(1, 5)
-    rs_dot(2, 2)
+    rs_dot(1, 5, 6)
     rs_send(1, 5)
-    rs_send(2, 2)
-    rs_dot(1, 6)
     rs_dot(2, 3)
     rs_send(1, 6)
     rs_send(2, 3)
-    rs_dot(2, 4, 5, 6)
+    finish(0)
+    rs_dot(2, 4)
     rs_send(2, 4)
     finish(1)
+    rs_dot(2, 5, 6)
+    attend(0, 0)
     rs_send(2, 5)
-    attend(0)
+    attend(0, 1)
     rs_send(2, 6)
     back_start(0)
     finish(2)
-    attend(1)
+    attend(1, 0, 1)
     back_finish(0)
     back_start(1)
     back_finish(1)
@@ -469,6 +474,7 @@
         pltpu.SMEM((3, 128), jnp.int32),
         vmem((2, TOKENS, 128), jnp.float32),
         vmem((2, TOKENS, 128), jnp.float32),
+        vmem((12, 2, HALF, 1024), bf),
         vmem((2, 64, CAP, HALF, 128), bf),
         vmem((64, CAP, HALF, 128), bf),
         vmem((64, CAP, HALF, 128), bf),
@@ -482,10 +488,10 @@
     for _ in range(2):
         for run in RUNS:
             scratch += [vmem((7, TOKENS, run[2] // 2), bf)] * 2
-    scratch += [vmem((12, h, 2, HALF, 128), bf) for h in GROUPS]
-    scratch += [vmem((8, 12, 2 * h, 128), bf) for h in GROUPS] * 2
-    scratch += [vmem((64, CAP, 2 * h, 128), bf) for h in GROUPS]
-    scratch += [vmem((8, 8, CAP, 2 * h, 128), bf) for h in GROUPS]
+    scratch += [vmem((12, HEADS, HALF, 128), bf)] * 2
+    scratch += [vmem((8, 12, HEADS, 128), bf)] * 4
+    scratch += [vmem((64, CAP, HEADS, 128), bf)] * 2
+    scratch += [vmem((8, 8, CAP, HEADS, 128), bf)] * 2
     dma = pltpu.SemaphoreType.DMA
     scratch += [
         dma((6,)),
@@ -502,10 +508,9 @@
     ]
     in_vmem = pl.BlockSpec(memory_space=pltpu.VMEM)
     anywhere = pl.BlockSpec(memory_space=pl.ANY)
-    heads = GROUPS[0]
     result = pl.pallas_call(
         kernel,
-        out_shape=jax.ShapeDtypeStruct((12, 8, N_GROUPS, 2 * heads, 128), bf),
+        out_shape=jax.ShapeDtypeStruct((12, 8, 2, HEADS, 128), bf),
         in_specs=[in_vmem] * 5 + [anywhere] * 5,
         out_specs=in_vmem,
         scratch_shapes=scratch,
@@ -517,14 +522,14 @@
         new_counts,
         cache_lengths,
         frequency,
-        new_rows.reshape(12, 2, HALF, 1024),
+        new_rows,
         query_weight,
         key_weight,
         value_weight,
         cache_keys,
         cache_values,
     )
-    return result.reshape(12, 64, 2, HEAD_DIM).transpose(0, 2, 1, 3).reshape(12, 2, 8192)
+    return result.transpose(0, 2, 1, 3, 4).reshape(12, 2, 8192)
 
 
 def solution(mesh):

time: 118 us -> 116 us (0.983)
  Pallas kernels: 116 us -> 113 us
    pallas_call x1, Pallas kernels: 116 us -> 113 us  [local(): pl.pallas_call(kernel, out_shape=jax.ShapeDtypeStruct((12, 8, 2, HEADS, 1...]
    unnamed x1 -> x0, local copies, waits for them, and re-layouts: 2.07 us -> none
where the time goes in v5:
time: 116 us; the launch traced here: 115 us
  Pallas kernels  113 us (97%)
  local copies, waits for them, and re-layouts  1.92 us (2%)
    pallas_call x1, Pallas kernels, local(): pl.pallas_call(kernel, out_shape=jax.ShapeDtypeStruct((12, 8, 2, HEADS, 1...  113 us

profile of v5, /device:TPU:1, one launch (start us, length us, event | category | flops | bytes accessed | tf_op | source)
XLA Modules:
  0.0 115.4 jit_solution(18301743136313269136)
XLA Ops:
  0.0 113.5 %shard_map.100 = bf16[12,8,2,8,128]{4,3,2,1,0:T(8,128)(2,1)} custom-call(s32[768]{0:T(1024)} %refs_0_.1, s32[768]{0:T(1024)} %refs_1_.1, s32[768]{0:T(1024)} %refs_2_.1, f32[1,128]{1,0:T(1,128)} %constant.2.clone.refs_3_, bf16[12,16,1024]{2,1,0:T(8,128)(2,1)} %refs_4_.1, bf16[1024,1024]{1,0:T(8,128)(2,1)} %refs_5_.1, bf16[1024,128]{1,0:T(8,128)(2,1)} %refs_6_.1, ...), custom_call_target="tpu_custom_call" | custom-call | tf_op jit(solution)/shard_map/pallas_call | solution.py:511
  113.5 1.1 copy.11
  114.6 0.8 reshape.3
